TPU v7x, 32 devices: a whole 2x2x4 slice. The times are simulated.
32 devices in a mesh: range: 32 (over z, y, x, core).
Axes of the slice: x: 2, y: 2, z: 4, core: 2. Of those that a mesh axis runs over, the one named last changes fastest.
Arguments:
- raw: bfloat16 [2, 64, 32, 8192], P(None, None, None, 'range'), may hold values from -40 to 40
- replica: bfloat16 [2, 128], replicated, may hold values from -1 to 1
- det_bin: int32 [1024], P('range'), may hold values from 0 to 31
- det_block: int32 [1024], P('range'), may hold values from 0 to 1
- det_beam: int32 [1024], P('range'), may hold values from 0 to 7
- det_owner: int32 [1024, 1], P('range'), may hold values from 0 to 31; in each aligned block of 32 rows (0 to 31, 32 to 63, ...) at most 2 rows name the same one
Outputs:
- tracked: float32 [2048, 256], P('range')
Inputs may be any that keep to these rules, and one draw needn't show every extreme that they name: `det_owner`: in each slab's detections no owner appears more than 2 times; some owner appears exactly 2 times.
All inputs are finite; a program needn't handle non-finite values.
Results may differ from a plain program's by a relative error of at most 0.025.
Values may be sent and summed in bfloat16 or wider, within the bound.
No kernel may reach another device: no remote copies, remote signals or barrier semaphores. Data moves between devices by JAX's collectives and lax.ppermute only.
A program may use at most 256 MiB of HBM per device.

v0:
```python
import functools
import math

import jax
import jax.numpy as jnp
import ml_dtypes
import numpy as np
from jax import lax
from jax.experimental import pallas as pl
from jax.experimental.pallas import tpu as pltpu
from jax.sharding import PartitionSpec as P

BLOCK = 128
BEAMS = 8
CAP = 2

F32 = jnp.float32
BF16 = jnp.bfloat16
VMEM = pltpu.VMEM
MIB = 1024 * 1024
NT = (((1,), (1,)), ((), ()))


def vmem_spec():
    return pl.BlockSpec(memory_space=VMEM)


def smem_spec():
    return pl.BlockSpec(memory_space=pltpu.SMEM)


def hbm_spec():
    return pl.BlockSpec(memory_space=pltpu.HBM)


def params(mib=16):
    return pltpu.CompilerParams(vmem_limit_bytes=mib * MIB)


def dot(a, b):
    return jnp.dot(a, b, preferred_element_type=F32)


def dot_nt(a, b, precision=None):
    return lax.dot_general(a, b, NT, precision=precision, preferred_element_type=F32)


def iota(shape, axis):
    return lax.broadcasted_iota(jnp.int32, shape, axis)


def halo_kernel(raw_ref, out_ref, buf, sems):
    parts = sems.shape[0]
    size = out_ref.shape[1] // parts
    copies = []
    for j in range(parts):
        rows = slice(j * size, (j + 1) * size)
        copies.append(
            pltpu.make_async_copy(raw_ref.at[:, rows, :], buf.at[:, rows, :], sems.at[j])
        )
    for copy in copies:
        copy.start()
    for j, copy in enumerate(copies):
        copy.wait()
        rows = slice(j * size, (j + 1) * size)
        out_ref[:, rows, :] = buf[:, rows, :BLOCK]


def first_gates(raw):
    return pl.pallas_call(
        halo_kernel,
        out_shape=jax.ShapeDtypeStruct(raw.shape[:2] + (BLOCK,), BF16),
        in_specs=[hbm_spec()],
        out_specs=vmem_spec(),
        scratch_shapes=[pltpu.VMEM(raw.shape, BF16), pltpu.SemaphoreType.DMA((8,))],
        compiler_params=params(63),
    )(raw)


def correlation_matrix(rep_ref, out_ref):
    taps = rep_ref.shape[1]
    base = rep_ref[...].astype(F32)
    row = iota((taps, 2 * taps), 0)
    parts = []
    for i in range(2):
        line = jnp.concatenate([base[i : i + 1], jnp.zeros((1, taps), F32)], axis=1)
        skew = jnp.broadcast_to(line, (taps, 2 * taps))
        bit = 1
        while bit < taps:
            skew = jnp.where((row & bit) != 0, pltpu.roll(skew, bit, 1), skew)
            bit *= 2
        parts.append(skew.T)
    real_part, imag_part = parts
    out_ref[0] = jnp.concatenate([real_part, -imag_part], axis=1).astype(BF16)
    out_ref[1] = jnp.concatenate([imag_part, real_part], axis=1).astype(BF16)


def doppler_matrix(pulses, group):
    index = np.arange(pulses)
    angle = 2.0 * math.pi / pulses * (index[:, None] * index[None, :] % pulses)
    cosine = np.cos(angle) * pulses**-0.5
    sine = np.sin(angle) * pulses**-0.5
    table = np.stack([np.stack([cosine, -sine], 1), np.stack([sine, cosine], 1)], 0)
    full = np.einsum("ipod,ce->dociep", table, np.eye(group))
    shape = (pulses * 2 * group, 2 * group * pulses)
    return full.reshape(shape).astype(ml_dtypes.bfloat16)


def doppler_rows(total, dft):
    compressed = total.astype(BF16)
    rows, wide = compressed.shape
    half, gates = rows // 2, wide // 2
    stacked = jnp.concatenate(
        [
            jnp.concatenate([compressed[:half, :gates], compressed[half:, :gates]], axis=1),
            jnp.concatenate([compressed[:half, gates:], compressed[half:, gates:]], axis=1),
        ],
        axis=0,
    )
    both = dot(dft, stacked)
    lines = both.shape[0] // 8
    joined = jnp.concatenate(
        [both[:, :gates].reshape(lines, 8, gates), both[:, gates:].reshape(lines, 8, gates)],
        axis=1,
    )
    return joined.astype(BF16)


GROUP = 16


def spectra_first_kernel(raw_ref, rep_ref, dft_ref, s_ref, local_ref, taps_ref, buf, sems):
    bins, _, chans, gates = s_ref.shape
    size = GROUP * bins
    copies = [
        pltpu.make_async_copy(
            raw_ref.at[:, j * size : (j + 1) * size, :],
            buf.at[:, j * size : (j + 1) * size, :],
            sems.at[j],
        )
        for j in range(chans // GROUP)
    ]
    for copy in copies:
        copy.start()
    correlation_matrix(rep_ref, taps_ref)
    for j, copy in enumerate(copies):
        copy.wait()
        rows = slice(j * size, (j + 1) * size)
        total = dot(buf[0, rows, :], taps_ref[0]) + dot(buf[1, rows, :], taps_ref[1])
        out = doppler_rows(total, dft_ref[...])
        s_ref[:, :, j * GROUP : (j + 1) * GROUP, :] = out.reshape(bins, 2, GROUP, gates)
        later = jnp.concatenate([buf[0, rows, gates:], buf[1, rows, gates:]], axis=1)
        near = jnp.concatenate([taps_ref[0, :gates, :], taps_ref[1, :gates, :]], axis=0)
        local_ref[rows, :] = dot(later, near)


def spectra_last_kernel(local_ref, halo_ref, taps_ref, dft_ref, s_ref):
    bins, _, chans, gates = s_ref.shape
    size = GROUP * bins
    for j in range(chans // GROUP):
        rows = slice(j * size, (j + 1) * size)
        later = jnp.concatenate([halo_ref[0, rows, :], halo_ref[1, rows, :]], axis=1)
        far = jnp.concatenate([taps_ref[0, gates:, :], taps_ref[1, gates:, :]], axis=0)
        out = doppler_rows(local_ref[rows, :] + dot(later, far), dft_ref[...])
        s_ref[:, :, j * GROUP : (j + 1) * GROUP, :] = out.reshape(bins, 2, GROUP, gates)


def spectra_first(raw, replica, table, pulses):
    _, rows, gates = raw.shape
    chans = rows // pulses
    taps = replica.shape[1]
    return pl.pallas_call(
        spectra_first_kernel,
        out_shape=[
            jax.ShapeDtypeStruct((pulses, 2, chans, BLOCK), BF16),
            jax.ShapeDtypeStruct((rows, 2 * BLOCK), F32),
            jax.ShapeDtypeStruct((2, 2 * taps, 2 * taps), BF16),
        ],
        in_specs=[hbm_spec(), vmem_spec(), vmem_spec()],
        out_specs=[vmem_spec()] * 3,
        scratch_shapes=[
            pltpu.VMEM(raw.shape, BF16),
            pltpu.SemaphoreType.DMA((chans // GROUP,)),
        ],
        compiler_params=params(),
    )(raw, replica, table)


def spectra_last(local, halo, matrix, table, pulses):
    rows = local.shape[0]
    return pl.pallas_call(
        spectra_last_kernel,
        out_shape=jax.ShapeDtypeStruct((pulses, 2, rows // pulses, BLOCK), BF16),
        in_specs=[vmem_spec()] * 4,
        out_specs=vmem_spec(),
        compiler_params=params(),
    )(local, halo, matrix, table)


def cross_body(base, s_ref, before_ref, out_ref):
    bins, _, chans, gates = s_ref.shape
    lower = iota((chans, chans), 0) >= iota((chans, chans), 1)
    half = chans // 2

    def packed(block):
        swapped = pltpu.roll(block, chans, 1)
        mixed = jnp.where(lower, block[:, :chans], swapped[:, :chans])
        return jnp.concatenate([mixed[:half], mixed[half:]], axis=1)

    def write(e, block):
        value = jnp.concatenate([packed(block[:chans]), block[chans:]], axis=0)
        if before_ref is not None:
            value = value + before_ref[base + e]
        out_ref[e] = value

    @pl.loop(0, out_ref.shape[0] // 2, unroll=2)
    def _(step):
        e = step * 2
        each = []
        for k in range(4):
            where = lax.rem(base + e + k, bins)
            each.append((s_ref[where, 0], s_ref[where, 1]))
        left = jnp.concatenate(
            [jnp.concatenate([re, im], axis=1) for re, im in each], axis=0
        )
        right = jnp.concatenate(
            [
                jnp.concatenate(pieces, axis=1)
                for re, im in each[:2]
                for pieces in ((re, im), (-im, re))
            ],
            axis=0,
        )
        both = dot_nt(left, right)
        write(e, both[: 3 * chans, : 2 * chans])
        write(e + 1, both[chans:, 2 * chans :])


def cross_first_kernel(s_ref, out_ref):
    cross_body(0, s_ref, None, out_ref)


def cross_last_kernel(mine, s_ref, before_ref, out_ref):
    core = lax.axis_index("range") & 1
    base = (core if mine else 1 - core) * out_ref.shape[0]
    cross_body(base, s_ref, before_ref, out_ref)


def cross_first(spectra):
    bins, _, chans, _ = spectra.shape
    return pl.pallas_call(
        cross_first_kernel,
        out_shape=jax.ShapeDtypeStruct((bins, 5 * chans // 2, 2 * chans), F32),
        in_specs=[vmem_spec()],
        out_specs=vmem_spec(),
        compiler_params=params(),
    )(spectra)


def cross_last(mine, spectra, before):
    bins = spectra.shape[0]
    return pl.pallas_call(
        functools.partial(cross_last_kernel, mine),
        out_shape=jax.ShapeDtypeStruct((bins // 2,) + before.shape[1:], F32),
        in_specs=[vmem_spec(), vmem_spec()],
        out_specs=vmem_spec(),
        compiler_params=params(),
    )(spectra, before)


def partner(value, bit):
    count = lax.axis_size("range")
    return lax.ppermute(value, "range", [(i, i ^ bit) for i in range(count)])


def slot_of(core, x, y, z):
    return (4 * z + ((2 * y + (x ^ y)) ^ (3 * (z & 1)))) ^ (15 * core)


def parts_of(index):
    return index & 1, (index >> 1) & 1, (index >> 2) & 1, (index >> 3) & 3


def bin_of(index):
    core, x, y, z = parts_of(index)
    return core * 16 + slot_of(core, x, y, z)


def index_of(bin_id):
    core = bin_id >> 4
    path = (bin_id & 15) ^ (15 * core)
    z = path >> 2
    turned = (path & 3) ^ (3 * (z & 1))
    y = turned >> 1
    x = (turned & 1) ^ y
    return z * 8 + y * 4 + x * 2 + core


def first_kernel(keep_ref, core_ref, a_ref, b_ref):
    core, x, y, z = parts_of(lax.axis_index("range"))
    half = keep_ref.shape[1] // 2
    for k in range(8):
        e = slot_of(core, 1 - x, k // 4, k % 4)
        a_ref[k] = keep_ref[e, :half] + core_ref[e, :half]
        e = slot_of(core, k // 4, 1 - y, k % 4)
        b_ref[k] = keep_ref[e, half:] + core_ref[e, half:]


def second_kernel(keep_ref, core_ref, a1_ref, b1_ref, a_ref, b_ref):
    core, x, y, z = parts_of(lax.axis_index("range"))
    half = keep_ref.shape[1] // 2
    for k in range(4):
        e = slot_of(core, x, 1 - y, k)
        a_ref[k] = keep_ref[e, :half] + core_ref[e, :half] + a1_ref[(1 - y) * 4 + k]
        e = slot_of(core, 1 - x, y, k)
        b_ref[k] = keep_ref[e, half:] + core_ref[e, half:] + b1_ref[(1 - x) * 4 + k]


def line_sum(keep_ref, core_ref, a1_ref, b1_ref, a2_ref, b2_ref, flip):
    core, x, y, z = parts_of(lax.axis_index("range"))
    z = z ^ flip
    half = keep_ref.shape[1] // 2
    e = slot_of(core, x, y, z)
    upper = keep_ref[e, :half] + core_ref[e, :half] + a1_ref[y * 4 + z] + a2_ref[z]
    lower = keep_ref[e, half:] + core_ref[e, half:] + b1_ref[x * 4 + z] + b2_ref[z]
    return upper, lower


def line_kernel(*refs):
    half = refs[0].shape[1] // 2
    for k, out_ref in enumerate(refs[6:]):
        upper, lower = line_sum(*refs[:6], k + 1)
        out_ref[:half] = upper
        out_ref[half:] = lower


def own_kernel(*refs):
    z1_ref, z2_ref, z3_ref, out_ref, packed_ref = refs[6:]
    half = refs[0].shape[1] // 2
    upper, lower = line_sum(*refs[:6], 0)
    upper = upper + z1_ref[:half] + (z2_ref[:half] + z3_ref[:half])
    out_ref[:half] = upper
    packed_ref[...] = upper[: packed_ref.shape[0]]
    out_ref[half:] = lower + z1_ref[half:] + (z2_ref[half:] + z3_ref[half:])


def summed(kernel, data, shapes):
    return pl.pallas_call(
        kernel,
        out_shape=[jax.ShapeDtypeStruct(shape, F32) for shape in shapes],
        in_specs=[vmem_spec()] * len(data),
        out_specs=[vmem_spec()] * len(shapes),
        compiler_params=params(),
    )(*data)


def bin_sums(keep, core):
    _, rows, wide = keep.shape
    half = rows // 2
    data = [keep, core]
    a, b = summed(first_kernel, data, [(8, half, wide)] * 2)
    data += [partner(a, 2), partner(b, 4)]
    a, b = summed(second_kernel, data, [(4, half, wide)] * 2)
    data += [partner(a, 4), partner(b, 2)]
    sends = summed(line_kernel, data, [(rows, wide)] * 3)
    data += [partner(value, (k + 1) * 8) for k, value in enumerate(sends)]
    own, packed = summed(own_kernel, data, [(rows, wide), (rows // 5, wide)])
    bit = 32
    while bit < lax.axis_size("range"):
        own = own + partner(own, bit)
        packed = packed + partner(packed, bit)
        bit *= 2
    return own, packed


def from_bin(value, offset):
    count = lax.axis_size("range")
    pairs = []
    for i in range(count):
        target = index_of((bin_of(i) - offset) % 32) | (i & ~31)
        pairs.append((i, target))
    return lax.ppermute(value, "range", pairs)


def turn(value):
    half = value.shape[1] // 2
    rolled = pltpu.roll(value, half, 1)
    return jnp.where(iota(value.shape, 1) < half, -rolled, rolled)


def embed(value):
    return jnp.concatenate([value, turn(value)], axis=0)


def mul(a, b):
    return jnp.dot(a, embed(b), precision=lax.Precision.HIGHEST, preferred_element_type=F32)


def mul_conj(a, b):
    half = a.shape[1] // 2
    stacked = jnp.concatenate([a, -turn(a)], axis=0)
    both = dot_nt(stacked, b, lax.Precision.HIGHEST)
    rows = a.shape[0]
    return jnp.concatenate([both[:rows], both[rows:]], axis=1)


def conj_mul(a, b):
    half = a.shape[1] // 2
    both = lax.dot_general(
        a, b, (((0,), (0,)), ((), ())),
        precision=lax.Precision.HIGHEST, preferred_element_type=F32,
    )
    return both[:half] - turn(both[half:])


def reciprocal(x):
    value = pl.reciprocal(x, approx=True)
    for _ in range(2):
        value = value * (2.0 - x * value)
    return value


def pivot_inverse(p):
    def times(x, y):
        return x[0] * y[0] - x[1] * y[1], x[0] * y[1] + x[1] * y[0]

    def conj(x):
        return x[0], -x[1]

    def plus(x, y):
        return x[0] + y[0], x[1] + y[1]

    def scaled(x, s):
        return x[0] * s, x[1] * s

    def square(x):
        return x[0] * x[0] + x[1] * x[1]

    def two(a, b, d):
        inv = reciprocal(a * d - square(b))
        return d * inv, scaled(b, -inv), a * inv

    a, d = p[0][0], p[1][1]
    b = p[0][1]
    ea, eb, ed = two(a, b, d)
    f = [[p[0][2], p[0][3]], [p[1][2], p[1][3]]]
    w = [
        [plus(scaled(f[0][j], ea), times(eb, f[1][j])) for j in range(2)],
        [plus(times(conj(eb), f[0][j]), scaled(f[1][j], ed)) for j in range(2)],
    ]

    def inner(i, j):
        return plus(times(conj(f[0][i]), w[0][j]), times(conj(f[1][i]), w[1][j]))

    ha = p[2][2] - inner(0, 0)[0]
    hd = p[3][3] - inner(1, 1)[0]
    cross = inner(0, 1)
    hb = (p[2][3][0] - cross[0], p[2][3][1] - cross[1])
    ga, gb, gd = two(ha, hb, hd)
    v = [
        [
            plus(scaled(w[i][0], ga), times(w[i][1], conj(gb))),
            plus(times(w[i][0], gb), scaled(w[i][1], gd)),
        ]
        for i in range(2)
    ]
    top = [
        [plus(times(v[i][0], conj(w[j][0])), times(v[i][1], conj(w[j][1]))) for j in range(2)]
        for i in range(2)
    ]
    zero = None
    out = [[None] * 4 for _ in range(4)]
    out[0][0] = (ea + top[0][0][0], zero)
    out[1][1] = (ed + top[1][1][0], zero)
    out[0][1] = plus(eb, top[0][1])
    out[2][2], out[3][3], out[2][3] = (ga, zero), (gd, zero), gb
    for i in range(2):
        for j in range(2):
            out[i][2 + j] = (-v[i][j][0], -v[i][j][1])
    for i in range(4):
        for j in range(i):
            out[i][j] = conj(out[j][i])
    return out


def invert(matrix):
    chans, width = matrix.shape
    sub = 8
    tiles = [matrix[t * sub : (t + 1) * sub, :] for t in range(chans // sub)]
    lane = iota((sub, width), 1)
    row = iota((sub, width), 0)
    first_half = lane < chans

    def spin(value):
        rolled = pltpu.roll(value, chans, 1)
        return jnp.where(first_half, -rolled, rolled)

    def column(value, k):
        return jnp.broadcast_to(value[:, k : k + 1], (sub, width))

    def combine(terms):
        while len(terms) > 1:
            terms = [
                terms[i] + terms[i + 1] if i + 1 < len(terms) else terms[i]
                for i in range(0, len(terms), 2)
            ]
        return terms[0]

    for k in range(0, chans, 4):
        t, r = divmod(k, sub)
        lines = [jnp.broadcast_to(tiles[t][r + i : r + i + 1, :], (sub, width)) for i in range(4)]
        pivot = [[None] * 4 for _ in range(4)]
        for i in range(4):
            pivot[i][i] = column(lines[i], k + i)
            for j in range(i + 1, 4):
                pivot[i][j] = column(lines[i], k + j), column(lines[i], chans + k + j)
        low = jnp.bitwise_and(lane, chans - 1)
        cleared = (low >= k) & (low < k + 4)
        unit = [
            jnp.where(cleared, jnp.where(lane == k + i, 1.0, 0.0), lines[i]) for i in range(4)
        ]
        spun = [spin(u) for u in unit]
        p = pivot_inverse(pivot)
        fresh_lines, fresh_spun = [], []
        for i in range(4):
            terms, other = [], []
            for j in range(4):
                re, im = p[i][j]
                terms.append(re * unit[j])
                other.append(re * spun[j])
                if im is not None:
                    terms.append(im * spun[j])
                    other.append(-(im * unit[j]))
            fresh_lines.append(combine(terms))
            fresh_spun.append(combine(other))
        fresh = []
        for s, tile in enumerate(tiles):
            terms = []
            for i in range(4):
                terms.append(column(tile, k + i) * fresh_lines[i])
                terms.append(column(tile, chans + k + i) * fresh_spun[i])
            value = jnp.where(cleared, 0.0, tile) - combine(terms)
            if s == t:
                for i in range(4):
                    value = jnp.where(row == r + i, fresh_lines[i], value)
            fresh.append(value)
        tiles = fresh
    return jnp.concatenate(tiles, axis=0)


def unpacked(ref, scale):
    half, wide = ref.shape[0], ref.shape[1]
    piece = ref[...] * scale
    swapped = pltpu.roll(piece, wide // 2, 1)
    return jnp.concatenate([piece, swapped], axis=0)[:, : wide // 2]


def hermitian(mixed, across):
    i, j = iota(mixed.shape, 0), iota(mixed.shape, 1)
    real_part = jnp.where(i >= j, mixed, across)
    imag_part = jnp.where(i < j, mixed, jnp.where(i > j, -across, 0.0))
    return jnp.concatenate([real_part, imag_part], axis=1)


def middle_kernel(total, packed_ref, steer_ref, inv_ref, t_ref):
    chans = inv_ref.shape[0]
    mixed = unpacked(packed_ref, F32(1.0 / total))
    twice = jnp.concatenate([mixed, mixed], axis=1)
    across = jnp.concatenate([twice, twice], axis=0).T[:chans, :chans]
    inverse = invert(hermitian(mixed, across))
    inv_ref[...] = inverse
    t_ref[...] = mul(steer_ref[...], inverse)


def outer_kernel(total, own_ref, left_ref, right_ref, steer_ref, inv_ref, t_ref, out_ref,
                 work, keep):
    chans = inv_ref.shape[0]
    scale = F32(1.0 / total)
    half = chans // 2
    m_left = unpacked(left_ref.at[:half], scale)
    m_right = unpacked(right_ref, scale)
    ml = left_ref[half : half + chans] * scale
    rl = left_ref[half + chans :] * scale
    rm = own_ref[half : half + chans] * scale
    pair = jnp.concatenate([m_left, m_right], axis=1)
    square = jnp.concatenate([pair, pair], axis=0).T
    inv_mid = inv_ref[...]
    t = t_ref[...]
    h = mul(inv_mid, ml)
    g = mul(rm, inv_mid)
    work[...] = hermitian(m_left, square[:chans, :chans]) - conj_mul(ml, h)
    s_rl = rl - mul(rm, h)
    s_rr = hermitian(m_right, square[chans:, :chans]) - mul_conj(g, rm)
    rhs_left = -mul(t, ml)
    rhs_right = -mul_conj(t, rm)
    keep[0] = s_rl
    keep[1] = s_rr
    keep[2] = h
    keep[3] = g
    keep[4, 0:BEAMS] = rhs_left
    keep[4, BEAMS : 2 * BEAMS] = rhs_right

    @pl.loop(0, 2)
    def _(stage):
        work[...] = invert(work[...])

        @pl.when(stage == 0)
        def _():
            inverse = work[...]
            s_rl = keep[0]
            both = mul(jnp.concatenate([s_rl, keep[4, 0:BEAMS]], axis=0), inverse)
            k, y_left = both[:chans], both[chans:]
            work[...] = keep[1] - mul_conj(k, s_rl)
            keep[0] = k
            keep[4, BEAMS : 2 * BEAMS] = keep[4, BEAMS : 2 * BEAMS] - mul_conj(y_left, s_rl)
            keep[4, 0:BEAMS] = y_left
            keep[4, 2 * BEAMS : 3 * BEAMS] = t_ref[...] - mul_conj(y_left, keep[2])
            keep[3] = keep[3] - mul_conj(k, keep[2])

        @pl.when(stage == 1)
        def _():
            y_right = mul(keep[4, BEAMS : 2 * BEAMS], work[...])
            y_left = keep[4, 0:BEAMS] - mul(y_right, keep[0])
            y_mid = keep[4, 2 * BEAMS : 3 * BEAMS] - mul(y_right, keep[3])
            quad = jnp.sum(steer_ref[...] * y_mid, axis=1, keepdims=True)
            y = jnp.concatenate([y_left, y_mid, y_right], axis=1) / jnp.sqrt(quad)
            real_lane = lax.rem(iota(y.shape, 1), 2 * chans) < chans
            mine = jnp.where(real_lane, y, -y).astype(BF16)
            for c in range(out_ref.shape[0]):
                out_ref[c] = mine


def steering(chans):
    index = np.arange(chans)
    sines = -0.8 + 1.6 * np.arange(BEAMS) / (BEAMS - 1)
    angle = math.pi * sines[:, None] * index[None, :]
    return np.concatenate([np.cos(angle), -np.sin(angle)], axis=1).astype(np.float32)


def solve_middle(packed, steer, total):
    half, wide = packed.shape
    return pl.pallas_call(
        functools.partial(middle_kernel, total),
        out_shape=[
            jax.ShapeDtypeStruct((2 * half, wide), F32),
            jax.ShapeDtypeStruct((BEAMS, wide), F32),
        ],
        in_specs=[vmem_spec()] * 2,
        out_specs=[vmem_spec()] * 2,
        compiler_params=params(),
    )(packed, steer)


def solve_outer(own, left, right, steer, inverse, t, total, copies):
    chans, wide = inverse.shape
    return pl.pallas_call(
        functools.partial(outer_kernel, total),
        out_shape=jax.ShapeDtypeStruct((copies, BEAMS, 3 * wide), BF16),
        in_specs=[vmem_spec()] * 6,
        out_specs=vmem_spec(),
        scratch_shapes=[pltpu.VMEM((chans, wide), F32), pltpu.VMEM((5, chans, wide), F32)],
        compiler_params=params(),
    )(own, left, right, steer, inverse, t)


def beam_kernel(bin_ref, block_ref, beam_ref, owner_ref, s0_ref, s1_ref, same_ref, other_ref,
                out_ref, both_ref, rows_ref, seen_ref):
    bins, wide, gates = s0_ref.shape
    devices = seen_ref.shape[0]
    count = bin_ref.shape[0]
    rows_ref[...] = jnp.zeros_like(rows_ref)

    @pl.loop(0, devices)
    def _(i):
        seen_ref[i] = 0

    core = lax.axis_index("range") & 1
    half = bins // 2
    for h, w_ref in enumerate((same_ref, other_ref)):
        w = w_ref[...].astype(F32).reshape(half * BEAMS, 3 * wide)
        lines = slice(h * half, (h + 1) * half)
        for k in range(3):
            lanes = slice(k * wide, (k + 1) * wide)
            part = w[:, lanes]
            both_ref[lines, 0:BEAMS, lanes] = part.reshape(half, BEAMS, wide)
            both_ref[lines, BEAMS:, lanes] = turn(part).reshape(half, BEAMS, wide)

    def detection(j, carry):
        bin_id = bin_ref[j]
        beam_id = beam_ref[j]
        owner = owner_ref[j]
        rank = seen_ref[owner]
        seen_ref[owner] = rank + 1
        index = index_of(bin_id)
        left = both_ref[(index >> 1) + half * ((index & 1) ^ core)].astype(BF16)
        bands = [lax.rem(bin_id + bins - 1 + k, bins) for k in range(3)]
        first = block_ref[j] == 0
        window = jnp.concatenate(
            [jnp.where(first, s0_ref[b], s1_ref[b]) for b in bands], axis=0
        )
        both = dot(left, window)
        line = jnp.concatenate([both[:BEAMS], both[BEAMS:]], axis=1)
        chosen = jnp.where(iota(line.shape, 0) == beam_id, line, 0.0)
        row = owner * CAP + rank
        rows_ref[pl.ds(row, 1), :] = jnp.sum(chosen, axis=0, keepdims=True)
        return carry

    lax.fori_loop(0, count, detection, 0, unroll=16)
    out_ref[...] = rows_ref[...].astype(BF16)


def beam_rows(det_bin, det_block, det_beam, owners, s0, s1, same, other, devices):
    bins, wide, gates = s0.shape
    return pl.pallas_call(
        beam_kernel,
        out_shape=jax.ShapeDtypeStruct((devices * CAP, 2 * gates), BF16),
        in_specs=[smem_spec()] * 4 + [vmem_spec()] * 4,
        out_specs=vmem_spec(),
        scratch_shapes=[
            pltpu.VMEM((bins, 2 * BEAMS, 3 * wide), F32),
            pltpu.VMEM((devices * CAP, 2 * gates), F32),
            pltpu.SMEM((devices,), jnp.int32),
        ],
        compiler_params=params(),
    )(det_bin, det_block, det_beam, owners, s0, s1, same, other)


def on_device(raw, replica, det_bin, det_block, det_beam, det_owner):
    devices = lax.axis_size("range")
    _, chans, pulses, gates = raw.shape
    bins = pulses
    flat = raw.reshape(2, chans * pulses, gates)
    halo = lax.ppermute(
        first_gates(flat), "range", [(source, source - 1) for source in range(1, devices)]
    )
    table = doppler_matrix(pulses, 8)
    s0, local, matrix = spectra_first(flat, replica, table, pulses)
    first = cross_first(s0)
    s1 = spectra_last(local, halo, matrix, table, pulses)
    core_sum = partner(cross_last(False, s1, first), 1)
    keep = cross_last(True, s1, first)
    own, packed = bin_sums(keep, core_sum)
    total = gates * devices
    steer = steering(chans)
    left = from_bin(own, -1)
    right = from_bin(packed, 1)
    inverse, t = solve_middle(packed, steer, total)
    mine = solve_outer(own, left, right, steer, inverse, t, total, bins // 2)
    groups = [
        [first + 2 * k + c for k in range(bins // 2)]
        for first in range(0, devices, bins) for c in range(2)
    ]
    same = lax.all_to_all(
        mine, "range", split_axis=0, concat_axis=0, tiled=True, axis_index_groups=groups
    )
    other = partner(same, 1)
    outgoing = beam_rows(
        det_bin, det_block, det_beam, det_owner[:, 0],
        s0.reshape(bins, 2 * chans, BLOCK), s1.reshape(bins, 2 * chans, BLOCK), same, other, devices,
    )
    incoming = lax.all_to_all(
        outgoing.reshape(devices, CAP, 2 * BLOCK), "range", split_axis=0, concat_axis=0, tiled=True
    )
    return incoming.astype(F32).reshape(devices * CAP, 2 * BLOCK)


def solution(mesh):
    in_specs = (
        P(None, None, None, "range"),
        P(),
        P("range"),
        P("range"),
        P("range"),
        P("range", None),
    )
    out_specs = P("range", None)
    return jax.shard_map(
        on_device, mesh=mesh, in_specs=in_specs, out_specs=out_specs, check_vma=False
    )
```

profile of v0, /device:TPU:0, one launch (start us, length us, event | category | flops | bytes accessed | tf_op | source)
XLA Modules:
  0.0 94.3 jit_solution(12567639251310655868)
XLA Ops:
  0.0 2.7 %shard_map.83 = bf16[2,2048,128]{2,1,0:T(8,128)(2,1)} custom-call(bf16[2,2048,256]{2,1,0:T(8,128)(2,1)} %bitcast.5), custom_call_target="tpu_custom_call" | custom-call | tf_op jit(solution)/shard_map/pallas_call | solution.py:70
  2.7 1.3 %collective-permute-start = (bf16[2,2048,128]{2,1,0:T(8,128)(2,1)}, bf16[2,2048,128]{2,1,0:T(8,128)(2,1)S(1)}, u32[]{:S(2)}, u32[]{:S(2)}) collective-permute-start(bf16[2,2048,128]{2,1,0:T(8,128)(2,1)} %shard_map.83), channel_id=1, source_target_pairs={{1,0},{2,1},{3,2},{4,3},{5,4},{6,5},{7,6},{8,7},{9,8},{10,9},{11,1... | collective-permute-start | bytes 3145736 | tf_op jit(solution)/shard_map/ppermute | solution.py:733
  4.0 1.6 %copy-done = bf16[2,64,32,256]{3,2,1,0:T(8,128)(2,1)S(1)} copy-done((bf16[2,64,32,256]{3,2,1,0:T(8,128)(2,1)S(1)}, bf16[2,64,32,256]{3,2,1,0:T(8,128)(2,1)}, u32[]{:S(2)}) %copy-start) | copy-done | bytes 2097176
  5.6 4.1 %shard_map.82 = (bf16[32,2,64,128]{3,2,1,0:T(8,128)(2,1)S(1)}, f32[2048,256]{1,0:T(8,128)S(1)}, bf16[2,256,256]{2,1,0:T(8,128)(2,1)S(1)}) custom-call(bf16[2,2048,256]{2,1,0:T(8,128)(2,1)S(1)} %bitcast.6, bf16[2,128]{1,0:T(2,128)(2,1)S(1)} %copy-done.3, bf16[512,512]{1,0:T(8,128)(2,1)S(1)} %copy-done.1), custom_call_target="tpu_custom_call" | custom-call | tf_op jit(solution)/shard_map/pallas_call | solution.py:172
  9.7 2.9 %shard_map.85.before_ref = f32[32,160,128]{2,1,0:T(8,128)S(1)} custom-call(bf16[32,2,64,128]{3,2,1,0:T(8,128)(2,1)S(1)} %get-tuple-element.19.s_ref), custom_call_target="tpu_custom_call" | custom-call | tf_op jit(solution)/shard_map/pallas_call | solution.py:251
  13.8 1.5 %shard_map.87 = f32[16,160,128]{2,1,0:T(8,128)S(1)} custom-call(bf16[32,2,64,128]{3,2,1,0:T(8,128)(2,1)S(1)} %shard_map.84.s_ref, f32[32,160,128]{2,1,0:T(8,128)S(1)} %shard_map.85.before_ref), custom_call_target="tpu_custom_call" | custom-call | tf_op jit(solution)/shard_map/pallas_call | solution.py:262
  15.3 7.8 %collective-permute-start.1 = (f32[16,160,128]{2,1,0:T(8,128)S(1)}, f32[16,160,128]{2,1,0:T(8,128)S(1)}, u32[]{:S(2)}, u32[]{:S(2)}) collective-permute-start(f32[16,160,128]{2,1,0:T(8,128)S(1)} %shard_map.87), channel_id=1, source_target_pairs={{0,1},{1,0},{2,3},{3,2},{4,5},{5,4},{6,7},{7,6},{8,9},{9,8},{10,11... | collective-permute-start | bytes 3932168 | tf_op jit(solution)/shard_map/ppermute | solution.py:273
  23.1 1.5 %shard_map.86.keep_ref.refs_0_ = f32[16,160,128]{2,1,0:T(8,128)S(1)} custom-call(bf16[32,2,64,128]{3,2,1,0:T(8,128)(2,1)S(1)} %shard_map.84.s_ref, f32[32,160,128]{2,1,0:T(8,128)S(1)} %shard_map.85.before_ref), custom_call_target="tpu_custom_call" | custom-call | tf_op jit(solution)/shard_map/pallas_call | solution.py:262
  25.8 2.4 %collective-permute-start.2 = (f32[8,80,128]{2,1,0:T(8,128)S(1)}, f32[8,80,128]{2,1,0:T(8,128)S(1)}, u32[]{:S(2)}, u32[]{:S(2)}) collective-permute-start(f32[8,80,128]{2,1,0:T(8,128)S(1)} %get-tuple-element.22), channel_id=1, source_target_pairs={{0,2},{1,3},{2,0},{3,1},{4,6},{5,7},{6,4},{7,5},{8,10},{9,11},{10,... | collective-permute-start | bytes 983048 | tf_op jit(solution)/shard_map/ppermute | solution.py:273
  28.3 2.4 %collective-permute-start.3 = (f32[8,80,128]{2,1,0:T(8,128)S(1)}, f32[8,80,128]{2,1,0:T(8,128)S(1)}, u32[]{:S(2)}, u32[]{:S(2)}) collective-permute-start(f32[8,80,128]{2,1,0:T(8,128)S(1)} %get-tuple-element.23), channel_id=1, source_target_pairs={{0,4},{1,5},{2,6},{3,7},{4,0},{5,1},{6,2},{7,3},{8,12},{9,13},{10,... | collective-permute-start | bytes 983048 | tf_op jit(solution)/shard_map/ppermute | solution.py:273
  30.7 5.8 %collective-permute-done.2.a1_ref.refs_2_ = f32[8,80,128]{2,1,0:T(8,128)S(1)} collective-permute-done((f32[8,80,128]{2,1,0:T(8,128)S(1)}, f32[8,80,128]{2,1,0:T(8,128)S(1)}, u32[]{:S(2)}, u32[]{:S(2)}) %collective-permute-start.2) | collective-permute-done | bytes 327712 | tf_op jit(solution)/shard_map/ppermute | solution.py:273
  36.5 2.1 %collective-permute-done.3.b1_ref.refs_3_ = f32[8,80,128]{2,1,0:T(8,128)S(1)} collective-permute-done((f32[8,80,128]{2,1,0:T(8,128)S(1)}, f32[8,80,128]{2,1,0:T(8,128)S(1)}, u32[]{:S(2)}, u32[]{:S(2)}) %collective-permute-start.3) | collective-permute-done | bytes 327712 | tf_op jit(solution)/shard_map/ppermute | solution.py:273
  38.7 1.8 %collective-permute-start.4 = (f32[4,80,128]{2,1,0:T(8,128)S(1)}, f32[4,80,128]{2,1,0:T(8,128)S(1)}, u32[]{:S(2)}, u32[]{:S(2)}) collective-permute-start(f32[4,80,128]{2,1,0:T(8,128)S(1)} %get-tuple-element.24), channel_id=1, source_target_pairs={{0,4},{1,5},{2,6},{3,7},{4,0},{5,1},{6,2},{7,3},{8,12},{9,13},{10,... | collective-permute-start | bytes 491528 | tf_op jit(solution)/shard_map/ppermute | solution.py:273
  40.9 3.6 %collective-permute-done.4.refs_4_ = f32[4,80,128]{2,1,0:T(8,128)S(1)} collective-permute-done((f32[4,80,128]{2,1,0:T(8,128)S(1)}, f32[4,80,128]{2,1,0:T(8,128)S(1)}, u32[]{:S(2)}, u32[]{:S(2)}) %collective-permute-start.4) | collective-permute-done | bytes 163872 | tf_op jit(solution)/shard_map/ppermute | solution.py:273
  44.4 1.4 %collective-permute-done.5.refs_5_ = f32[4,80,128]{2,1,0:T(8,128)S(1)} collective-permute-done((f32[4,80,128]{2,1,0:T(8,128)S(1)}, f32[4,80,128]{2,1,0:T(8,128)S(1)}, u32[]{:S(2)}, u32[]{:S(2)}) %collective-permute-start.5) | collective-permute-done | bytes 163872 | tf_op jit(solution)/shard_map/ppermute | solution.py:273
  45.9 1.6 %collective-permute-start.6 = (f32[160,128]{1,0:T(8,128)S(1)}, f32[160,128]{1,0:T(8,128)S(1)}, u32[]{:S(2)}, u32[]{:S(2)}) collective-permute-start(f32[160,128]{1,0:T(8,128)S(1)} %get-tuple-element.26), channel_id=1, source_target_pairs={{0,8},{1,9},{2,10},{3,11},{4,12},{5,13},{6,14},{7,15},{8,0},{9,1},... | collective-permute-start | bytes 245768 | tf_op jit(solution)/shard_map/ppermute | solution.py:273
  48.6 1.8 %collective-permute-start.8 = (f32[160,128]{1,0:T(8,128)S(1)}, f32[160,128]{1,0:T(8,128)S(1)}, u32[]{:S(2)}, u32[]{:S(2)}) collective-permute-start(f32[160,128]{1,0:T(8,128)S(1)} %get-tuple-element.28), channel_id=1, source_target_pairs={{0,24},{1,25},{2,26},{3,27},{4,28},{5,29},{6,30},{7,31},{8,16},{9,... | collective-permute-start | bytes 245768 | tf_op jit(solution)/shard_map/ppermute | solution.py:273
  50.5 4.5 %collective-permute-done.7.refs_7_ = f32[160,128]{1,0:T(8,128)S(1)} collective-permute-done((f32[160,128]{1,0:T(8,128)S(1)}, f32[160,128]{1,0:T(8,128)S(1)}, u32[]{:S(2)}, u32[]{:S(2)}) %collective-permute-start.7) | collective-permute-done | bytes 81952 | tf_op jit(solution)/shard_map/ppermute | solution.py:273
  55.8 4.0 %shard_map.92 = (f32[64,128]{1,0:T(8,128)S(1)}, f32[8,128]{1,0:T(8,128)S(1)}) custom-call(f32[32,128]{1,0:T(8,128)S(1)} %get-tuple-element.30.packed_ref, f32[8,128]{1,0:T(8,128)S(1)} %copy-done.2), custom_call_target="tpu_custom_call" | custom-call | tf_op jit(solution)/shard_map/pallas_call | solution.py:642
  59.8 8.6 %shard_map.93 = bf16[16,8,384]{2,1,0:T(8,128)(2,1)S(1)} custom-call(f32[160,128]{1,0:T(8,128)S(1)} %get-tuple-element.29.own_ref, f32[160,128]{1,0:T(8,128)S(1)} %collective-permute-done.9.left_ref, f32[32,128]{1,0:T(8,128)S(1)} %collective-permute-done.10.right_ref, f32[8,128]{1,0:T(8,128)S(1)} %copy-done.2, f32[64,128]{1,0:T(8,128)S(1)} %get-tuple-element.31.inv_ref, ...), custom_call_target="tpu_custom_call" | custom-call | tf_op jit(solution)/shard_map/pallas_call | solution.py:656
  68.4 12.8 %all_to_all.10.same_ref = bf16[16,8,384]{2,1,0:T(8,128)(2,1)S(1)} all-to-all(bf16[16,8,384]{2,1,0:T(8,128)(2,1)S(1)} %shard_map.93), channel_id=1, replica_groups={{0,2,4,6,8,10,12,14,16,18,20,22,24,26,28,30},{1,3,5,7,9,11,13,15,17,19,..., dimensions={0} | all-to-all | bytes 196608 | tf_op jit(solution)/shard_map/all_to_all | solution.py:753
  81.2 1.3 %collective-permute-done.11.other_ref = bf16[16,8,384]{2,1,0:T(8,128)(2,1)S(1)} collective-permute-done((bf16[16,8,384]{2,1,0:T(8,128)(2,1)S(1)}, bf16[16,8,384]{2,1,0:T(8,128)(2,1)S(1)}, u32[]{:S(2)}, u32[]{:S(2)}) %collective-permute-start.11) | collective-permute-done | bytes 98336 | tf_op jit(solution)/shard_map/ppermute | solution.py:273
  82.5 2.1 %shard_map.94 = bf16[64,256]{1,0:T(8,128)(2,1)S(1)} custom-call(s32[32]{0:T(128)S(1)} %copy-done.4, s32[32]{0:T(128)S(1)} %copy-done.5, s32[32]{0:T(128)S(1)} %copy-done.6, s32[32]{0:T(128)S(1)} %bitcast.8, bf16[32,128,128]{2,1,0:T(8,128)(2,1)S(1)} %bitcast.7, bf16[32,128,128]{2,1,0:T(8,128)(2,1)S(1)} %bitcast.4, ...), custom_call_target="tpu_custom_call" | custom-call | tf_op jit(solution)/shard_map/pallas_call | solution.py:714
  84.7 8.9 %all_to_all.11 = bf16[32,2,256]{2,1,0:T(2,128)(2,1)S(1)} all-to-all(bf16[32,2,256]{2,1,0:T(2,128)(2,1)S(1)} %reshape.21), channel_id=1, replica_groups=mesh['range'=32] {'range'}, dimensions={0} | all-to-all | bytes 65536 | tf_op jit(solution)/shard_map/all_to_all | solution.py:761
  (33 shorter events, 5.7 us)
Async XLA Ops:
  0.0 4.0 %copy-start.1 = (bf16[512,512]{1,0:T(8,128)(2,1)S(1)}, bf16[512,512]{1,0:T(8,128)(2,1)}, u32[]{:S(2)}) copy-start(bf16[512,512]{1,0:T(8,128)(2,1)} %constant.4.clone.dft_ref) | copy-start | bytes 1572868
  0.0 4.0 %copy-start.3 = (bf16[2,128]{1,0:T(2,128)(2,1)S(1)}, bf16[2,128]{1,0:T(2,128)(2,1)}, u32[]{:S(2)}) copy-start(bf16[2,128]{1,0:T(2,128)(2,1)} %rep_ref.1) | copy-start | bytes 1540
  2.7 9.9 %collective-permute-start = (bf16[2,2048,128]{2,1,0:T(8,128)(2,1)}, bf16[2,2048,128]{2,1,0:T(8,128)(2,1)S(1)}, u32[]{:S(2)}, u32[]{:S(2)}) collective-permute-start(bf16[2,2048,128]{2,1,0:T(8,128)(2,1)} %shard_map.83), channel_id=1, source_target_pairs={{1,0},{2,1},{3,2},{4,3},{5,4},{6,5},{7,6},{8,7},{9,8},{10,9},{11,1... | collective-permute-start | bytes 3145736 | tf_op jit(solution)/shard_map/ppermute | solution.py:733
  4.0 1.6 %copy-start = (bf16[2,64,32,256]{3,2,1,0:T(8,128)(2,1)S(1)}, bf16[2,64,32,256]{3,2,1,0:T(8,128)(2,1)}, u32[]{:S(2)}) copy-start(bf16[2,64,32,256]{3,2,1,0:T(8,128)(2,1)} %param.8) | copy-start | bytes 6291460
  15.3 10.4 %collective-permute-start.1 = (f32[16,160,128]{2,1,0:T(8,128)S(1)}, f32[16,160,128]{2,1,0:T(8,128)S(1)}, u32[]{:S(2)}, u32[]{:S(2)}) collective-permute-start(f32[16,160,128]{2,1,0:T(8,128)S(1)} %shard_map.87), channel_id=1, source_target_pairs={{0,1},{1,0},{2,3},{3,2},{4,5},{5,4},{6,7},{7,6},{8,9},{9,8},{10,11... | collective-permute-start | bytes 3932168 | tf_op jit(solution)/shard_map/ppermute | solution.py:273
  25.8 10.7 %collective-permute-start.2 = (f32[8,80,128]{2,1,0:T(8,128)S(1)}, f32[8,80,128]{2,1,0:T(8,128)S(1)}, u32[]{:S(2)}, u32[]{:S(2)}) collective-permute-start(f32[8,80,128]{2,1,0:T(8,128)S(1)} %get-tuple-element.22), channel_id=1, source_target_pairs={{0,2},{1,3},{2,0},{3,1},{4,6},{5,7},{6,4},{7,5},{8,10},{9,11},{10,... | collective-permute-start | bytes 983048 | tf_op jit(solution)/shard_map/ppermute | solution.py:273
  28.3 10.4 %collective-permute-start.3 = (f32[8,80,128]{2,1,0:T(8,128)S(1)}, f32[8,80,128]{2,1,0:T(8,128)S(1)}, u32[]{:S(2)}, u32[]{:S(2)}) collective-permute-start(f32[8,80,128]{2,1,0:T(8,128)S(1)} %get-tuple-element.23), channel_id=1, source_target_pairs={{0,4},{1,5},{2,6},{3,7},{4,0},{5,1},{6,2},{7,3},{8,12},{9,13},{10,... | collective-permute-start | bytes 983048 | tf_op jit(solution)/shard_map/ppermute | solution.py:273
  38.7 5.7 %collective-permute-start.4 = (f32[4,80,128]{2,1,0:T(8,128)S(1)}, f32[4,80,128]{2,1,0:T(8,128)S(1)}, u32[]{:S(2)}, u32[]{:S(2)}) collective-permute-start(f32[4,80,128]{2,1,0:T(8,128)S(1)} %get-tuple-element.24), channel_id=1, source_target_pairs={{0,4},{1,5},{2,6},{3,7},{4,0},{5,1},{6,2},{7,3},{8,12},{9,13},{10,... | collective-permute-start | bytes 491528 | tf_op jit(solution)/shard_map/ppermute | solution.py:273
  40.5 5.3 %collective-permute-start.5 = (f32[4,80,128]{2,1,0:T(8,128)S(1)}, f32[4,80,128]{2,1,0:T(8,128)S(1)}, u32[]{:S(2)}, u32[]{:S(2)}) collective-permute-start(f32[4,80,128]{2,1,0:T(8,128)S(1)} %get-tuple-element.25), channel_id=1, source_target_pairs={{0,2},{1,3},{2,0},{3,1},{4,6},{5,7},{6,4},{7,5},{8,10},{9,11},{10,... | collective-permute-start | bytes 491528 | tf_op jit(solution)/shard_map/ppermute | solution.py:273
  45.9 9.9 %copy-start.2 = (f32[8,128]{1,0:T(8,128)S(1)}, f32[8,128]{1,0:T(8,128)}, u32[]{:S(2)}) copy-start(f32[8,128]{1,0:T(8,128)} %constant.5.clone.steer_ref) | copy-start | bytes 12292
  45.9 4.6 %collective-permute-start.6 = (f32[160,128]{1,0:T(8,128)S(1)}, f32[160,128]{1,0:T(8,128)S(1)}, u32[]{:S(2)}, u32[]{:S(2)}) collective-permute-start(f32[160,128]{1,0:T(8,128)S(1)} %get-tuple-element.26), channel_id=1, source_target_pairs={{0,8},{1,9},{2,10},{3,11},{4,12},{5,13},{6,14},{7,15},{8,0},{9,1},... | collective-permute-start | bytes 245768 | tf_op jit(solution)/shard_map/ppermute | solution.py:273
  47.5 7.5 %collective-permute-start.7 = (f32[160,128]{1,0:T(8,128)S(1)}, f32[160,128]{1,0:T(8,128)S(1)}, u32[]{:S(2)}, u32[]{:S(2)}) collective-permute-start(f32[160,128]{1,0:T(8,128)S(1)} %get-tuple-element.27), channel_id=1, source_target_pairs={{0,16},{1,17},{2,18},{3,19},{4,20},{5,21},{6,22},{7,23},{8,24},{9,... | collective-permute-start | bytes 245768 | tf_op jit(solution)/shard_map/ppermute | solution.py:273
  48.6 33.9 %copy-start.4 = (s32[32]{0:T(128)S(1)}, s32[32]{0:T(128)}, u32[]{:S(2)}) copy-start(s32[32]{0:T(128)} %bin_ref.1) | copy-start | bytes 388
  48.6 33.9 %copy-start.5 = (s32[32]{0:T(128)S(1)}, s32[32]{0:T(128)}, u32[]{:S(2)}) copy-start(s32[32]{0:T(128)} %block_ref.1) | copy-start | bytes 388
  48.6 33.9 %copy-start.6 = (s32[32]{0:T(128)S(1)}, s32[32]{0:T(128)}, u32[]{:S(2)}) copy-start(s32[32]{0:T(128)} %beam_ref.1) | copy-start | bytes 388
  48.6 33.9 %copy-start.7 = (s32[32,1]{0,1:T(1,128)S(1)}, s32[32,1]{0,1:T(1,128)}, u32[]{:S(2)}) copy-start(s32[32,1]{0,1:T(1,128)} %param.13) | copy-start | bytes 388
  48.6 6.4 %collective-permute-start.8 = (f32[160,128]{1,0:T(8,128)S(1)}, f32[160,128]{1,0:T(8,128)S(1)}, u32[]{:S(2)}, u32[]{:S(2)}) collective-permute-start(f32[160,128]{1,0:T(8,128)S(1)} %get-tuple-element.28), channel_id=1, source_target_pairs={{0,24},{1,25},{2,26},{3,27},{4,28},{5,29},{6,30},{7,31},{8,16},{9,... | collective-permute-start | bytes 245768 | tf_op jit(solution)/shard_map/ppermute | solution.py:273
  55.0 4.7 %collective-permute-start.9 = (f32[160,128]{1,0:T(8,128)S(1)}, f32[160,128]{1,0:T(8,128)S(1)}, u32[]{:S(2)}, u32[]{:S(2)}) collective-permute-start(f32[160,128]{1,0:T(8,128)S(1)} %get-tuple-element.29.own_ref), channel_id=1, source_target_pairs={{0,2},{1,0},{2,6},{3,1},{4,12},{5,7},{6,4},{7,3},{8,16},{9,11},{10... | collective-permute-start | bytes 245768 | tf_op jit(solution)/shard_map/ppermute | solution.py:382
  55.8 4.0 %collective-permute-start.10 = (f32[32,128]{1,0:T(8,128)S(1)}, f32[32,128]{1,0:T(8,128)S(1)}, u32[]{:S(2)}, u32[]{:S(2)}) collective-permute-start(f32[32,128]{1,0:T(8,128)S(1)} %get-tuple-element.30.packed_ref), channel_id=1, source_target_pairs={{0,1},{1,3},{2,0},{3,7},{4,6},{5,13},{6,2},{7,5},{8,10},{9,17},{10... | collective-permute-start | bytes 49160 | tf_op jit(solution)/shard_map/ppermute | solution.py:382
  81.2 1.3 %collective-permute-start.11 = (bf16[16,8,384]{2,1,0:T(8,128)(2,1)S(1)}, bf16[16,8,384]{2,1,0:T(8,128)(2,1)S(1)}, u32[]{:S(2)}, u32[]{:S(2)}) collective-permute-start(bf16[16,8,384]{2,1,0:T(8,128)(2,1)S(1)} %all_to_all.10.same_ref), channel_id=1, source_target_pairs={{0,1},{1,0},{2,3},{3,2},{4,5},{5,4},{6,7},{7,6},{8,9},{9,8},{10,11... | collective-permute-start | bytes 294920 | tf_op jit(solution)/shard_map/ppermute | solution.py:273
where the time goes:
time: 94.5 us; the launch traced here: 94.3 us
  Pallas kernels  28.7 us (30%)
  blocking collectives  21.8 us (23%)
  starting transfers between devices  21.3 us (23%)
  waiting for transfers between devices  20 us (21%)
  local copies, waits for them, and re-layouts  2.27 us (2%)
    ppermute x9, waiting for transfers between devices, partner(): return lax.ppermute(value, 'range', [(i, i ^ bit) for i in range(count)])  20 us
    ppermute x9, starting transfers between devices, partner(): return lax.ppermute(value, 'range', [(i, i ^ bit) for i in range(count)])  19.3 us
    all_to_all x1, blocking collectives, on_device(): lax.all_to_all(mine, 'range', split_axis=0, concat_axis=0, tiled=True, ax...  12.8 us
    all_to_all x1, blocking collectives, on_device(): lax.all_to_all(outgoing.reshape(devices, CAP, 2 * BLOCK), 'range', split_...  8.95 us
    pallas_call x1, Pallas kernels, solve_outer(): pl.pallas_call(functools.partial(outer_kernel, total), out_shape=jax.Shap...  8.57 us
    pallas_call x1, Pallas kernels, spectra_first(): pl.pallas_call(spectra_first_kernel, out_shape=[jax.ShapeDtypeStruct((pul...  4.08 us
    pallas_call x1, Pallas kernels, solve_middle(): pl.pallas_call(functools.partial(middle_kernel, total), out_shape=[jax.Sh...  4 us
    pallas_call x2, Pallas kernels, cross_last(): pl.pallas_call(functools.partial(cross_last_kernel, mine), out_shape=jax....  2.92 us
  transfers between devices with their start and end apart: 12, of which 8 were waited for; matrix products, arithmetic and copies ran while one was open for 0% of the time, Pallas kernels for 13%

commit v1 on v0

--- a/solution.py
+++ b/solution.py
@@ -49,30 +49,31 @@
     return lax.broadcasted_iota(jnp.int32, shape, axis)
 
 
-def halo_kernel(raw_ref, out_ref, buf, sems):
-    parts = sems.shape[0]
-    size = out_ref.shape[1] // parts
-    copies = []
-    for j in range(parts):
-        rows = slice(j * size, (j + 1) * size)
-        copies.append(
-            pltpu.make_async_copy(raw_ref.at[:, rows, :], buf.at[:, rows, :], sems.at[j])
+def halo_kernel(part, parts, raw_ref, out_ref, sems):
+    count = sems.shape[0]
+    size = out_ref.shape[1] // count
+    start = part * (raw_ref.shape[1] // parts)
+    copies = [
+        pltpu.make_async_copy(
+            raw_ref.at[:, start + j * size : start + (j + 1) * size, :BLOCK],
+            out_ref.at[:, j * size : (j + 1) * size, :],
+            sems.at[j],
         )
+        for j in range(count)
+    ]
     for copy in copies:
         copy.start()
-    for j, copy in enumerate(copies):
+    for copy in copies:
         copy.wait()
-        rows = slice(j * size, (j + 1) * size)
-        out_ref[:, rows, :] = buf[:, rows, :BLOCK]
-
-
-def first_gates(raw):
+
+
+def first_gates(raw, part, parts):
     return pl.pallas_call(
-        halo_kernel,
-        out_shape=jax.ShapeDtypeStruct(raw.shape[:2] + (BLOCK,), BF16),
+        functools.partial(halo_kernel, part, parts),
+        out_shape=jax.ShapeDtypeStruct((2, raw.shape[1] // parts, BLOCK), BF16),
         in_specs=[hbm_spec()],
         out_specs=vmem_spec(),
-        scratch_shapes=[pltpu.VMEM(raw.shape, BF16), pltpu.SemaphoreType.DMA((8,))],
+        scratch_shapes=[pltpu.SemaphoreType.DMA((4,))],
         compiler_params=params(63),
     )(raw)
 
@@ -129,7 +130,17 @@
 GROUP = 16
 
 
-def spectra_first_kernel(raw_ref, rep_ref, dft_ref, s_ref, local_ref, taps_ref, buf, sems):
+def half_of_bins(bins, mine):
+    core = lax.axis_index("range") & 1
+    return (core if mine else 1 - core) * (bins // 2)
+
+
+def sent_bins(bins):
+    return bins // 2 + 2
+
+
+def spectra_first_kernel(raw_ref, rep_ref, dft_ref, s_ref, local_ref, taps_ref, send_ref,
+                         buf, sems):
     bins, _, chans, gates = s_ref.shape
     size = GROUP * bins
     copies = [
@@ -152,17 +163,45 @@
         later = jnp.concatenate([buf[0, rows, gates:], buf[1, rows, gates:]], axis=1)
         near = jnp.concatenate([taps_ref[0, :gates, :], taps_ref[1, :gates, :]], axis=0)
         local_ref[rows, :] = dot(later, near)
-
-
-def spectra_last_kernel(local_ref, halo_ref, taps_ref, dft_ref, s_ref):
-    bins, _, chans, gates = s_ref.shape
+    base = half_of_bins(bins, False)
+    for k in range(send_ref.shape[0]):
+        send_ref[k] = s_ref[lax.rem(base + k, bins)]
+
+
+def spectra_part(part, local_ref, halo_ref, taps_ref, dft_ref, bins, gates, write):
     size = GROUP * bins
-    for j in range(chans // GROUP):
+    count = halo_ref.shape[1] // size
+    far = jnp.concatenate([taps_ref[0, gates:, :], taps_ref[1, gates:, :]], axis=0)
+    for j in range(count):
         rows = slice(j * size, (j + 1) * size)
         later = jnp.concatenate([halo_ref[0, rows, :], halo_ref[1, rows, :]], axis=1)
-        far = jnp.concatenate([taps_ref[0, gates:, :], taps_ref[1, gates:, :]], axis=0)
-        out = doppler_rows(local_ref[rows, :] + dot(later, far), dft_ref[...])
-        s_ref[:, :, j * GROUP : (j + 1) * GROUP, :] = out.reshape(bins, 2, GROUP, gates)
+        place = part * count + j
+        near = local_ref[place * size : (place + 1) * size, :]
+        out = doppler_rows(near + dot(later, far), dft_ref[...])
+        write(j, out.reshape(bins, 2, GROUP, gates))
+
+
+def spectra_upper_kernel(local_ref, halo_ref, taps_ref, dft_ref, _, s_ref):
+    bins, _, _, gates = s_ref.shape
+
+    def write(j, value):
+        s_ref[:, :, j * GROUP : (j + 1) * GROUP, :] = value
+
+    spectra_part(0, local_ref, halo_ref, taps_ref, dft_ref, bins, gates, write)
+
+
+def spectra_lower_kernel(upper_ref, local_ref, halo_ref, taps_ref, dft_ref, s_ref, send_ref):
+    bins, _, chans, gates = s_ref.shape
+    half = upper_ref.shape[2]
+    s_ref[:, :, :half, :] = upper_ref[...]
+
+    def write(j, value):
+        s_ref[:, :, half + j * GROUP : half + (j + 1) * GROUP, :] = value
+
+    spectra_part(1, local_ref, halo_ref, taps_ref, dft_ref, bins, gates, write)
+    base = half_of_bins(bins, False)
+    for k in range(send_ref.shape[0]):
+        send_ref[k] = s_ref[lax.rem(base + k, bins)]
 
 
 def spectra_first(raw, replica, table, pulses):
@@ -175,9 +214,10 @@
             jax.ShapeDtypeStruct((pulses, 2, chans, BLOCK), BF16),
             jax.ShapeDtypeStruct((rows, 2 * BLOCK), F32),
             jax.ShapeDtypeStruct((2, 2 * taps, 2 * taps), BF16),
+            jax.ShapeDtypeStruct((sent_bins(pulses), 2, chans, BLOCK), BF16),
         ],
         in_specs=[hbm_spec(), vmem_spec(), vmem_spec()],
-        out_specs=[vmem_spec()] * 3,
+        out_specs=[vmem_spec()] * 4,
         scratch_shapes=[
             pltpu.VMEM(raw.shape, BF16),
             pltpu.SemaphoreType.DMA((chans // GROUP,)),
@@ -186,19 +226,33 @@
     )(raw, replica, table)
 
 
-def spectra_last(local, halo, matrix, table, pulses):
-    rows = local.shape[0]
-    return pl.pallas_call(
-        spectra_last_kernel,
-        out_shape=jax.ShapeDtypeStruct((pulses, 2, rows // pulses, BLOCK), BF16),
-        in_specs=[vmem_spec()] * 4,
+def spectra_last(local, halos, matrix, table, pulses, sums):
+    chans = local.shape[0] // pulses
+    upper = pl.pallas_call(
+        spectra_upper_kernel,
+        out_shape=jax.ShapeDtypeStruct((pulses, 2, chans // 2, BLOCK), BF16),
+        in_specs=[vmem_spec()] * 4 + [pl.BlockSpec(memory_space=pl.ANY)],
         out_specs=vmem_spec(),
         compiler_params=params(),
-    )(local, halo, matrix, table)
-
-
-def cross_body(base, s_ref, before_ref, out_ref):
-    bins, _, chans, gates = s_ref.shape
+    )(local, halos[0], matrix, table, sums)
+    return pl.pallas_call(
+        spectra_lower_kernel,
+        out_shape=[
+            jax.ShapeDtypeStruct((pulses, 2, chans, BLOCK), BF16),
+            jax.ShapeDtypeStruct((sent_bins(pulses), 2, chans, BLOCK), BF16),
+        ],
+        in_specs=[vmem_spec()] * 5,
+        out_specs=[vmem_spec()] * 2,
+        compiler_params=params(),
+    )(upper, local, halos[1], matrix, table)
+
+
+def cross_kernel(s_ref, *refs):
+    before_ref = refs[0] if len(refs) == 2 else None
+    out_ref = refs[-1]
+    held, _, chans, gates = s_ref.shape
+    count = out_ref.shape[0]
+    base = half_of_bins(held, True) if held == 2 * count else 0
     lower = iota((chans, chans), 0) >= iota((chans, chans), 1)
     half = chans // 2
 
@@ -210,15 +264,15 @@
     def write(e, block):
         value = jnp.concatenate([packed(block[:chans]), block[chans:]], axis=0)
         if before_ref is not None:
-            value = value + before_ref[base + e]
+            value = value + before_ref[e]
         out_ref[e] = value
 
-    @pl.loop(0, out_ref.shape[0] // 2, unroll=2)
+    @pl.loop(0, count // 2, unroll=2)
     def _(step):
         e = step * 2
         each = []
         for k in range(4):
-            where = lax.rem(base + e + k, bins)
+            where = lax.rem(base + e + k, held)
             each.append((s_ref[where, 0], s_ref[where, 1]))
         left = jnp.concatenate(
             [jnp.concatenate([re, im], axis=1) for re, im in each], axis=0
@@ -236,36 +290,16 @@
         write(e + 1, both[chans:, 2 * chans :])
 
 
-def cross_first_kernel(s_ref, out_ref):
-    cross_body(0, s_ref, None, out_ref)
-
-
-def cross_last_kernel(mine, s_ref, before_ref, out_ref):
-    core = lax.axis_index("range") & 1
-    base = (core if mine else 1 - core) * out_ref.shape[0]
-    cross_body(base, s_ref, before_ref, out_ref)
-
-
-def cross_first(spectra):
-    bins, _, chans, _ = spectra.shape
+def cross(spectra, bins, before=None):
+    chans = spectra.shape[2]
+    data = [spectra] if before is None else [spectra, before]
     return pl.pallas_call(
-        cross_first_kernel,
-        out_shape=jax.ShapeDtypeStruct((bins, 5 * chans // 2, 2 * chans), F32),
-        in_specs=[vmem_spec()],
+        cross_kernel,
+        out_shape=jax.ShapeDtypeStruct((bins // 2, 5 * chans // 2, 2 * chans), F32),
+        in_specs=[vmem_spec()] * len(data),
         out_specs=vmem_spec(),
         compiler_params=params(),
-    )(spectra)
-
-
-def cross_last(mine, spectra, before):
-    bins = spectra.shape[0]
-    return pl.pallas_call(
-        functools.partial(cross_last_kernel, mine),
-        out_shape=jax.ShapeDtypeStruct((bins // 2,) + before.shape[1:], F32),
-        in_specs=[vmem_spec(), vmem_spec()],
-        out_specs=vmem_spec(),
-        compiler_params=params(),
-    )(spectra, before)
+    )(*data)
 
 
 def partner(value, bit):
@@ -296,48 +330,48 @@
     return z * 8 + y * 4 + x * 2 + core
 
 
-def first_kernel(keep_ref, core_ref, a_ref, b_ref):
+def first_kernel(keep_ref, a_ref, b_ref):
     core, x, y, z = parts_of(lax.axis_index("range"))
     half = keep_ref.shape[1] // 2
     for k in range(8):
         e = slot_of(core, 1 - x, k // 4, k % 4)
-        a_ref[k] = keep_ref[e, :half] + core_ref[e, :half]
+        a_ref[k] = keep_ref[e, :half]
         e = slot_of(core, k // 4, 1 - y, k % 4)
-        b_ref[k] = keep_ref[e, half:] + core_ref[e, half:]
-
-
-def second_kernel(keep_ref, core_ref, a1_ref, b1_ref, a_ref, b_ref):
+        b_ref[k] = keep_ref[e, half:]
+
+
+def second_kernel(keep_ref, a1_ref, b1_ref, a_ref, b_ref):
     core, x, y, z = parts_of(lax.axis_index("range"))
     half = keep_ref.shape[1] // 2
     for k in range(4):
         e = slot_of(core, x, 1 - y, k)
-        a_ref[k] = keep_ref[e, :half] + core_ref[e, :half] + a1_ref[(1 - y) * 4 + k]
+        a_ref[k] = keep_ref[e, :half] + a1_ref[(1 - y) * 4 + k]
         e = slot_of(core, 1 - x, y, k)
-        b_ref[k] = keep_ref[e, half:] + core_ref[e, half:] + b1_ref[(1 - x) * 4 + k]
-
-
-def line_sum(keep_ref, core_ref, a1_ref, b1_ref, a2_ref, b2_ref, flip):
+        b_ref[k] = keep_ref[e, half:] + b1_ref[(1 - x) * 4 + k]
+
+
+def line_sum(keep_ref, a1_ref, b1_ref, a2_ref, b2_ref, flip):
     core, x, y, z = parts_of(lax.axis_index("range"))
     z = z ^ flip
     half = keep_ref.shape[1] // 2
     e = slot_of(core, x, y, z)
-    upper = keep_ref[e, :half] + core_ref[e, :half] + a1_ref[y * 4 + z] + a2_ref[z]
-    lower = keep_ref[e, half:] + core_ref[e, half:] + b1_ref[x * 4 + z] + b2_ref[z]
+    upper = keep_ref[e, :half] + a1_ref[y * 4 + z] + a2_ref[z]
+    lower = keep_ref[e, half:] + b1_ref[x * 4 + z] + b2_ref[z]
     return upper, lower
 
 
 def line_kernel(*refs):
     half = refs[0].shape[1] // 2
-    for k, out_ref in enumerate(refs[6:]):
-        upper, lower = line_sum(*refs[:6], k + 1)
+    for k, out_ref in enumerate(refs[5:]):
+        upper, lower = line_sum(*refs[:5], k + 1)
         out_ref[:half] = upper
         out_ref[half:] = lower
 
 
 def own_kernel(*refs):
-    z1_ref, z2_ref, z3_ref, out_ref, packed_ref = refs[6:]
+    z1_ref, z2_ref, z3_ref, out_ref, packed_ref = refs[5:]
     half = refs[0].shape[1] // 2
-    upper, lower = line_sum(*refs[:6], 0)
+    upper, lower = line_sum(*refs[:5], 0)
     upper = upper + z1_ref[:half] + (z2_ref[:half] + z3_ref[:half])
     out_ref[:half] = upper
     packed_ref[...] = upper[: packed_ref.shape[0]]
@@ -354,10 +388,10 @@
     )(*data)
 
 
-def bin_sums(keep, core):
+def bin_sums(keep):
     _, rows, wide = keep.shape
     half = rows // 2
-    data = [keep, core]
+    data = [keep]
     a, b = summed(first_kernel, data, [(8, half, wide)] * 2)
     data += [partner(a, 2), partner(b, 4)]
     a, b = summed(second_kernel, data, [(4, half, wide)] * 2)
@@ -663,8 +697,8 @@
     )(own, left, right, steer, inverse, t)
 
 
-def beam_kernel(bin_ref, block_ref, beam_ref, owner_ref, s0_ref, s1_ref, same_ref, other_ref,
-                out_ref, both_ref, rows_ref, seen_ref):
+def beam_kernel(bin_ref, block_ref, beam_ref, owner_ref, s0_ref, s1_ref, w_ref, out_ref,
+                both_ref, rows_ref, seen_ref):
     bins, wide, gates = s0_ref.shape
     devices = seen_ref.shape[0]
     count = bin_ref.shape[0]
@@ -674,16 +708,12 @@
     def _(i):
         seen_ref[i] = 0
 
-    core = lax.axis_index("range") & 1
-    half = bins // 2
-    for h, w_ref in enumerate((same_ref, other_ref)):
-        w = w_ref[...].astype(F32).reshape(half * BEAMS, 3 * wide)
-        lines = slice(h * half, (h + 1) * half)
-        for k in range(3):
-            lanes = slice(k * wide, (k + 1) * wide)
-            part = w[:, lanes]
-            both_ref[lines, 0:BEAMS, lanes] = part.reshape(half, BEAMS, wide)
-            both_ref[lines, BEAMS:, lanes] = turn(part).reshape(half, BEAMS, wide)
+    w = w_ref[...].astype(F32).reshape(bins * BEAMS, 3 * wide)
+    for k in range(3):
+        lanes = slice(k * wide, (k + 1) * wide)
+        part = w[:, lanes]
+        both_ref[:, 0:BEAMS, lanes] = part.reshape(bins, BEAMS, wide)
+        both_ref[:, BEAMS:, lanes] = turn(part).reshape(bins, BEAMS, wide)
 
     def detection(j, carry):
         bin_id = bin_ref[j]
@@ -691,8 +721,7 @@
         owner = owner_ref[j]
         rank = seen_ref[owner]
         seen_ref[owner] = rank + 1
-        index = index_of(bin_id)
-        left = both_ref[(index >> 1) + half * ((index & 1) ^ core)].astype(BF16)
+        left = both_ref[index_of(bin_id)].astype(BF16)
         bands = [lax.rem(bin_id + bins - 1 + k, bins) for k in range(3)]
         first = block_ref[j] == 0
         window = jnp.concatenate(
@@ -709,12 +738,12 @@
     out_ref[...] = rows_ref[...].astype(BF16)
 
 
-def beam_rows(det_bin, det_block, det_beam, owners, s0, s1, same, other, devices):
+def beam_rows(det_bin, det_block, det_beam, owners, s0, s1, weight, devices):
     bins, wide, gates = s0.shape
     return pl.pallas_call(
         beam_kernel,
         out_shape=jax.ShapeDtypeStruct((devices * CAP, 2 * gates), BF16),
-        in_specs=[smem_spec()] * 4 + [vmem_spec()] * 4,
+        in_specs=[smem_spec()] * 4 + [vmem_spec()] * 3,
         out_specs=vmem_spec(),
         scratch_shapes=[
             pltpu.VMEM((bins, 2 * BEAMS, 3 * wide), F32),
@@ -722,7 +751,7 @@
             pltpu.SMEM((devices,), jnp.int32),
         ],
         compiler_params=params(),
-    )(det_bin, det_block, det_beam, owners, s0, s1, same, other)
+    )(det_bin, det_block, det_beam, owners, s0, s1, weight)
 
 
 def on_device(raw, replica, det_bin, det_block, det_beam, det_owner):
@@ -730,33 +759,32 @@
     _, chans, pulses, gates = raw.shape
     bins = pulses
     flat = raw.reshape(2, chans * pulses, gates)
-    halo = lax.ppermute(
-        first_gates(flat), "range", [(source, source - 1) for source in range(1, devices)]
-    )
+    before = [(source, source - 1) for source in range(1, devices)]
+    halos = [lax.ppermute(first_gates(flat, part, 2), "range", before) for part in range(2)]
     table = doppler_matrix(pulses, 8)
-    s0, local, matrix = spectra_first(flat, replica, table, pulses)
-    first = cross_first(s0)
-    s1 = spectra_last(local, halo, matrix, table, pulses)
-    core_sum = partner(cross_last(False, s1, first), 1)
-    keep = cross_last(True, s1, first)
-    own, packed = bin_sums(keep, core_sum)
+    s0, local, matrix, send0 = spectra_first(flat, replica, table, pulses)
+    beside0 = partner(send0, 1)
+    sums = cross(s0, bins)
+    sums = cross(beside0, bins, sums)
+    s1, send1 = spectra_last(local, halos, matrix, table, pulses, sums)
+    beside1 = partner(send1, 1)
+    sums = cross(s1, bins, sums)
+    sums = cross(beside1, bins, sums)
+    own, packed = bin_sums(sums)
     total = gates * devices
     steer = steering(chans)
     left = from_bin(own, -1)
     right = from_bin(packed, 1)
     inverse, t = solve_middle(packed, steer, total)
-    mine = solve_outer(own, left, right, steer, inverse, t, total, bins // 2)
-    groups = [
-        [first + 2 * k + c for k in range(bins // 2)]
-        for first in range(0, devices, bins) for c in range(2)
-    ]
-    same = lax.all_to_all(
-        mine, "range", split_axis=0, concat_axis=0, tiled=True, axis_index_groups=groups
+    mine = solve_outer(own, left, right, steer, inverse, t, total, bins)
+    groups = [list(range(first, first + bins)) for first in range(0, devices, bins)]
+    weight = lax.all_to_all(
+        mine, "range", split_axis=0, concat_axis=0, tiled=True,
+        axis_index_groups=groups if len(groups) > 1 else None,
     )
-    other = partner(same, 1)
     outgoing = beam_rows(
         det_bin, det_block, det_beam, det_owner[:, 0],
-        s0.reshape(bins, 2 * chans, BLOCK), s1.reshape(bins, 2 * chans, BLOCK), same, other, devices,
+        s0.reshape(bins, 2 * chans, BLOCK), s1.reshape(bins, 2 * chans, BLOCK), weight, devices,
     )
     incoming = lax.all_to_all(
         outgoing.reshape(devices, CAP, 2 * BLOCK), "range", split_axis=0, concat_axis=0, tiled=True

time: 94.5 us -> 103 us (1.090)
  local copies, waits for them, and re-layouts: 2.27 us -> 7.68 us
  Pallas kernels: 28.7 us -> 32 us
  starting transfers between devices: 21.3 us -> 22.4 us
    unnamed x16 -> x28, local copies, waits for them, and re-layouts: 1.61 us -> 7.02 us
    pallas_call x5 -> x8, Pallas kernels: 9.72 us -> 12.2 us  [the longest x4 5.84 us: cross(): pl.pallas_call(cross_kernel, out_shape=jax.ShapeDtypeStruct((bins // 2, 5...]
    ppermute x1 -> x2, starting transfers between devices: 1.29 us -> 2.58 us  [on_device(): lax.ppermute(first_gates(flat, part, 2), 'range', before)]
    all_to_all x1, blocking collectives: 12.8 us -> 11.7 us  [on_device(): lax.all_to_all(mine, 'range', split_axis=0, concat_axis=0, tiled=True, ax...]
  transfers between devices with their start and end apart: 12 -> 13, of which waited for: 8 -> 8; matrix products, arithmetic and copies ran while one was open for 0% -> 0% of each run, Pallas kernels for 13% -> 14%
where the time goes in v1:
time: 103 us
  Pallas kernels  32 us (31%)
  starting transfers between devices  22.4 us (22%)
  blocking collectives  21.5 us (21%)
  waiting for transfers between devices  19 us (18%)
  local copies, waits for them, and re-layouts  7.68 us (7%)
    ppermute x9, starting transfers between devices, partner(): return lax.ppermute(value, 'range', [(i, i ^ bit) for i in range(count)])  19.3 us
    ppermute x9, waiting for transfers between devices, partner(): return lax.ppermute(value, 'range', [(i, i ^ bit) for i in range(count)])  19 us
    all_to_all x1, blocking collectives, on_device(): lax.all_to_all(mine, 'range', split_axis=0, concat_axis=0, tiled=True, ax...  11.7 us
    all_to_all x1, blocking collectives, on_device(): lax.all_to_all(outgoing.reshape(devices, CAP, 2 * BLOCK), 'range', split_...  9.77 us
    pallas_call x1, Pallas kernels, solve_outer(): pl.pallas_call(functools.partial(outer_kernel, total), out_shape=jax.Shap...  8.58 us
    unnamed x28, local copies, waits for them, and re-layouts  7.02 us
    pallas_call x4, Pallas kernels, cross(): pl.pallas_call(cross_kernel, out_shape=jax.ShapeDtypeStruct((bins // 2, 5...  5.84 us
    pallas_call x1, Pallas kernels, spectra_first(): pl.pallas_call(spectra_first_kernel, out_shape=[jax.ShapeDtypeStruct((pul...  4.94 us
  transfers between devices with their start and end apart: 13, of which 8 were waited for; matrix products, arithmetic and copies ran while one was open for 0% of the time, Pallas kernels for 14%

profile of v1, /device:TPU:0, one launch (start us, length us, event | category | flops | bytes accessed | tf_op | source)
XLA Modules:
  0.0 102.8 jit_solution(13517518846017083352)
XLA Ops:
  0.0 1.6 %copy-done = bf16[2,64,32,256]{3,2,1,0:T(8,128)(2,1)S(1)} copy-done((bf16[2,64,32,256]{3,2,1,0:T(8,128)(2,1)S(1)}, bf16[2,64,32,256]{3,2,1,0:T(8,128)(2,1)}, u32[]{:S(2)}) %copy-start) | copy-done | bytes 2097176
  3.3 4.9 %shard_map.82 = (bf16[32,2,64,128]{3,2,1,0:T(8,128)(2,1)S(1)}, f32[2048,256]{1,0:T(8,128)S(1)}, bf16[2,256,256]{2,1,0:T(8,128)(2,1)S(1)}, bf16[18,2,64,128]{3,2,1,0:T(8,128)(2,1)}) custom-call(bf16[2,2048,256]{2,1,0:T(8,128)(2,1)S(1)} %bitcast.6, bf16[2,128]{1,0:T(2,128)(2,1)S(1)} %copy-done.9, bf16[512,512]{1,0:T(8,128)(2,1)S(1)} %copy-done.3), custom_call_target="tpu_custom_call" | custom-call | tf_op jit(solution)/shard_map/pallas_call | solution.py:211
  11.0 1.9 %shard_map.83 = bf16[2,1024,128]{2,1,0:T(8,128)(2,1)} custom-call(bf16[2,2048,256]{2,1,0:T(8,128)(2,1)} %bitcast.4), custom_call_target="tpu_custom_call" | custom-call | tf_op jit(solution)/shard_map/pallas_call | solution.py:71
  14.3 1.9 %shard_map.87 = bf16[2,1024,128]{2,1,0:T(8,128)(2,1)} custom-call(bf16[2,2048,256]{2,1,0:T(8,128)(2,1)} %bitcast.5), custom_call_target="tpu_custom_call" | custom-call | tf_op jit(solution)/shard_map/pallas_call | solution.py:71
  20.2 1.5 %shard_map.85._.refs_0_ = f32[16,160,128]{2,1,0:T(8,128)S(1)} custom-call(bf16[18,2,64,128]{3,2,1,0:T(8,128)(2,1)S(1)} %collective-permute-done.1.s_ref, f32[16,160,128]{2,1,0:T(8,128)S(1)} %shard_map.84.refs_0_), custom_call_target="tpu_custom_call" | custom-call | tf_op jit(solution)/shard_map/pallas_call | solution.py:296
  21.9 1.7 %shard_map.86.upper_ref = bf16[32,2,32,128]{3,2,1,0:T(8,128)(2,1)S(1)} custom-call(f32[2048,256]{1,0:T(8,128)S(1)} %copy-done.2, bf16[2,1024,128]{2,1,0:T(8,128)(2,1)} %collective-permute-done.halo_ref, bf16[2,256,256]{2,1,0:T(8,128)(2,1)S(1)} %get-tuple-element.24.taps_ref, bf16[512,512]{1,0:T(8,128)(2,1)S(1)} %copy-done.4, ...), custom_call_target="tpu_custom_call" | custom-call | tf_op jit(solution)/shard_map/pallas_call | solution.py:231
  24.4 6.6 %collective-permute-start.3 = (bf16[18,2,64,128]{3,2,1,0:T(8,128)(2,1)S(1)}, bf16[18,2,64,128]{3,2,1,0:T(8,128)(2,1)S(1)}, u32[]{:S(2)}, u32[]{:S(2)}) collective-permute-start(bf16[18,2,64,128]{3,2,1,0:T(8,128)(2,1)S(1)} %get-tuple-element.27), channel_id=1, source_target_pairs={{0,1},{1,0},{2,3},{3,2},{4,5},{5,4},{6,7},{7,6},{8,9},{9,8},{10,11... | collective-permute-start | bytes 1769480 | tf_op jit(solution)/shard_map/ppermute | solution.py:307
  31.0 1.5 %shard_map.89.refs_0_ = f32[16,160,128]{2,1,0:T(8,128)S(1)} custom-call(bf16[32,2,64,128]{3,2,1,0:T(8,128)(2,1)S(1)} %get-tuple-element.26.s_ref, f32[16,160,128]{2,1,0:T(8,128)S(1)} %shard_map.85._.refs_0_), custom_call_target="tpu_custom_call" | custom-call | tf_op jit(solution)/shard_map/pallas_call | solution.py:296
  32.7 1.5 %shard_map.90.keep_ref.refs_0_ = f32[16,160,128]{2,1,0:T(8,128)S(1)} custom-call(bf16[18,2,64,128]{3,2,1,0:T(8,128)(2,1)S(1)} %collective-permute-done.3.s_ref, f32[16,160,128]{2,1,0:T(8,128)S(1)} %shard_map.89.refs_0_), custom_call_target="tpu_custom_call" | custom-call | tf_op jit(solution)/shard_map/pallas_call | solution.py:296
  34.2 3.1 %collective-permute-start.4 = (f32[8,80,128]{2,1,0:T(8,128)S(1)}, f32[8,80,128]{2,1,0:T(8,128)S(1)}, u32[]{:S(2)}, u32[]{:S(2)}) collective-permute-start(f32[8,80,128]{2,1,0:T(8,128)S(1)} %get-tuple-element.28), channel_id=1, source_target_pairs={{0,2},{1,3},{2,0},{3,1},{4,6},{5,7},{6,4},{7,5},{8,10},{9,11},{10,... | collective-permute-start | bytes 983048 | tf_op jit(solution)/shard_map/ppermute | solution.py:307
  37.3 2.4 %collective-permute-start.5 = (f32[8,80,128]{2,1,0:T(8,128)S(1)}, f32[8,80,128]{2,1,0:T(8,128)S(1)}, u32[]{:S(2)}, u32[]{:S(2)}) collective-permute-start(f32[8,80,128]{2,1,0:T(8,128)S(1)} %get-tuple-element.29), channel_id=1, source_target_pairs={{0,4},{1,5},{2,6},{3,7},{4,0},{5,1},{6,2},{7,3},{8,12},{9,13},{10,... | collective-permute-start | bytes 983048 | tf_op jit(solution)/shard_map/ppermute | solution.py:307
  39.7 5.8 %collective-permute-done.4.a1_ref.refs_1_ = f32[8,80,128]{2,1,0:T(8,128)S(1)} collective-permute-done((f32[8,80,128]{2,1,0:T(8,128)S(1)}, f32[8,80,128]{2,1,0:T(8,128)S(1)}, u32[]{:S(2)}, u32[]{:S(2)}) %collective-permute-start.4) | collective-permute-done | bytes 327712 | tf_op jit(solution)/shard_map/ppermute | solution.py:307
  45.5 2.1 %collective-permute-done.5.b1_ref.refs_2_ = f32[8,80,128]{2,1,0:T(8,128)S(1)} collective-permute-done((f32[8,80,128]{2,1,0:T(8,128)S(1)}, f32[8,80,128]{2,1,0:T(8,128)S(1)}, u32[]{:S(2)}, u32[]{:S(2)}) %collective-permute-start.5) | collective-permute-done | bytes 327712 | tf_op jit(solution)/shard_map/ppermute | solution.py:307
  47.7 1.8 %collective-permute-start.6 = (f32[4,80,128]{2,1,0:T(8,128)S(1)}, f32[4,80,128]{2,1,0:T(8,128)S(1)}, u32[]{:S(2)}, u32[]{:S(2)}) collective-permute-start(f32[4,80,128]{2,1,0:T(8,128)S(1)} %get-tuple-element.30), channel_id=1, source_target_pairs={{0,4},{1,5},{2,6},{3,7},{4,0},{5,1},{6,2},{7,3},{8,12},{9,13},{10,... | collective-permute-start | bytes 491528 | tf_op jit(solution)/shard_map/ppermute | solution.py:307
  49.9 3.6 %collective-permute-done.6.refs_3_ = f32[4,80,128]{2,1,0:T(8,128)S(1)} collective-permute-done((f32[4,80,128]{2,1,0:T(8,128)S(1)}, f32[4,80,128]{2,1,0:T(8,128)S(1)}, u32[]{:S(2)}, u32[]{:S(2)}) %collective-permute-start.6) | collective-permute-done | bytes 163872 | tf_op jit(solution)/shard_map/ppermute | solution.py:307
  54.9 1.6 %collective-permute-start.10 = (f32[160,128]{1,0:T(8,128)S(1)}, f32[160,128]{1,0:T(8,128)S(1)}, u32[]{:S(2)}, u32[]{:S(2)}) collective-permute-start(f32[160,128]{1,0:T(8,128)S(1)} %get-tuple-element.34), channel_id=1, source_target_pairs={{0,24},{1,25},{2,26},{3,27},{4,28},{5,29},{6,30},{7,31},{8,16},{9,... | collective-permute-start | bytes 245768 | tf_op jit(solution)/shard_map/ppermute | solution.py:307
  56.5 1.6 %collective-permute-start.8 = (f32[160,128]{1,0:T(8,128)S(1)}, f32[160,128]{1,0:T(8,128)S(1)}, u32[]{:S(2)}, u32[]{:S(2)}) collective-permute-start(f32[160,128]{1,0:T(8,128)S(1)} %get-tuple-element.32), channel_id=1, source_target_pairs={{0,8},{1,9},{2,10},{3,11},{4,12},{5,13},{6,14},{7,15},{8,0},{9,1},... | collective-permute-start | bytes 245768 | tf_op jit(solution)/shard_map/ppermute | solution.py:307
  59.5 1.9 %collective-permute-done.10.refs_7_ = f32[160,128]{1,0:T(8,128)S(1)} collective-permute-done((f32[160,128]{1,0:T(8,128)S(1)}, f32[160,128]{1,0:T(8,128)S(1)}, u32[]{:S(2)}, u32[]{:S(2)}) %collective-permute-start.10) | collective-permute-done | bytes 81952 | tf_op jit(solution)/shard_map/ppermute | solution.py:307
  62.4 2.9 %collective-permute-done.9.refs_6_ = f32[160,128]{1,0:T(8,128)S(1)} collective-permute-done((f32[160,128]{1,0:T(8,128)S(1)}, f32[160,128]{1,0:T(8,128)S(1)}, u32[]{:S(2)}, u32[]{:S(2)}) %collective-permute-start.9) | collective-permute-done | bytes 81952 | tf_op jit(solution)/shard_map/ppermute | solution.py:307
  66.0 4.0 %shard_map.95 = (f32[64,128]{1,0:T(8,128)S(1)}, f32[8,128]{1,0:T(8,128)S(1)}) custom-call(f32[32,128]{1,0:T(8,128)S(1)} %get-tuple-element.36.packed_ref, f32[8,128]{1,0:T(8,128)S(1)} %copy-done.8), custom_call_target="tpu_custom_call" | custom-call | tf_op jit(solution)/shard_map/pallas_call | solution.py:676
  70.0 8.6 %shard_map.96 = bf16[32,8,384]{2,1,0:T(8,128)(2,1)S(1)} custom-call(f32[160,128]{1,0:T(8,128)S(1)} %get-tuple-element.35.own_ref, f32[160,128]{1,0:T(8,128)S(1)} %collective-permute-done.11.left_ref, f32[32,128]{1,0:T(8,128)S(1)} %collective-permute-done.12.right_ref, f32[8,128]{1,0:T(8,128)S(1)} %copy-done.8, f32[64,128]{1,0:T(8,128)S(1)} %get-tuple-element.37.inv_ref, ...), custom_call_target="tpu_custom_call" | custom-call | tf_op jit(solution)/shard_map/pallas_call | solution.py:690
  78.6 11.7 %all_to_all.10.w_ref = bf16[32,8,384]{2,1,0:T(8,128)(2,1)S(1)} all-to-all(bf16[32,8,384]{2,1,0:T(8,128)(2,1)S(1)} %shard_map.96), channel_id=1, replica_groups=mesh['range'=32] {'range'}, dimensions={0} | all-to-all | bytes 393216 | tf_op jit(solution)/shard_map/all_to_all | solution.py:781
  90.3 2.1 %shard_map.97 = bf16[64,256]{1,0:T(8,128)(2,1)S(1)} custom-call(s32[32]{0:T(128)S(1)} %copy-done.10, s32[32]{0:T(128)S(1)} %copy-done.11, s32[32]{0:T(128)S(1)} %copy-done.12, s32[32]{0:T(128)S(1)} %bitcast.9, bf16[32,128,128]{2,1,0:T(8,128)(2,1)S(1)} %bitcast.8, bf16[32,128,128]{2,1,0:T(8,128)(2,1)S(1)} %bitcast.7, bf16[32,8,384]{2,1,0:T(8,128)(2,1)S(1)} %all_to_all.10.w_ref), custom_call_target="tpu_custom_call" | custom-call | tf_op jit(solution)/shard_map/pallas_call | solution.py:743
  92.4 9.8 %all_to_all.11 = bf16[32,2,256]{2,1,0:T(2,128)(2,1)S(1)} all-to-all(bf16[32,2,256]{2,1,0:T(2,128)(2,1)S(1)} %reshape.21), channel_id=1, replica_groups=mesh['range'=32] {'range'}, dimensions={0} | all-to-all | bytes 65536 | tf_op jit(solution)/shard_map/all_to_all | solution.py:789
  (50 shorter events, 16.5 us)
Async XLA Ops:
  0.0 1.6 %copy-start = (bf16[2,64,32,256]{3,2,1,0:T(8,128)(2,1)S(1)}, bf16[2,64,32,256]{3,2,1,0:T(8,128)(2,1)}, u32[]{:S(2)}) copy-start(bf16[2,64,32,256]{3,2,1,0:T(8,128)(2,1)} %param.8) | copy-start | bytes 6291460
  8.2 1.4 %copy-start.1 = (f32[2048,256]{1,0:T(8,128)}, f32[2048,256]{1,0:T(8,128)S(1)}, u32[]{:S(2)}) copy-start(f32[2048,256]{1,0:T(8,128)S(1)} %get-tuple-element.23.local_ref) | copy-start | bytes 6291460
  10.6 9.7 %collective-permute-start.1 = (bf16[18,2,64,128]{3,2,1,0:T(8,128)(2,1)}, bf16[18,2,64,128]{3,2,1,0:T(8,128)(2,1)S(1)}, u32[]{:S(2)}, u32[]{:S(2)}) collective-permute-start(bf16[18,2,64,128]{3,2,1,0:T(8,128)(2,1)} %get-tuple-element.25), channel_id=1, source_target_pairs={{0,1},{1,0},{2,3},{3,2},{4,5},{5,4},{6,7},{7,6},{8,9},{9,8},{10,11... | collective-permute-start | bytes 1769480 | tf_op jit(solution)/shard_map/ppermute | solution.py:307
  13.0 8.8 %collective-permute-start = (bf16[2,1024,128]{2,1,0:T(8,128)(2,1)}, bf16[2,1024,128]{2,1,0:T(8,128)(2,1)}, u32[]{:S(2)}, u32[]{:S(2)}) collective-permute-start(bf16[2,1024,128]{2,1,0:T(8,128)(2,1)} %shard_map.83), channel_id=1, source_target_pairs={{1,0},{2,1},{3,2},{4,3},{5,4},{6,5},{7,6},{8,7},{9,8},{10,9},{11,1... | collective-permute-start | bytes 1572872 | tf_op jit(solution)/shard_map/ppermute | solution.py:763
  16.2 7.4 %collective-permute-start.2 = (bf16[2,1024,128]{2,1,0:T(8,128)(2,1)}, bf16[2,1024,128]{2,1,0:T(8,128)(2,1)S(1)}, u32[]{:S(2)}, u32[]{:S(2)}) collective-permute-start(bf16[2,1024,128]{2,1,0:T(8,128)(2,1)} %shard_map.87), channel_id=1, source_target_pairs={{1,0},{2,1},{3,2},{4,3},{5,4},{6,5},{7,6},{8,7},{9,8},{10,9},{11,1... | collective-permute-start | bytes 1572872 | tf_op jit(solution)/shard_map/ppermute | solution.py:763
  17.5 1.2 %copy-start.6 = (bf16[32,2,64,128]{3,2,1,0:T(8,128)(2,1)S(1)}, bf16[32,2,64,128]{3,2,1,0:T(8,128)(2,1)}, u32[]{:S(2)}) copy-start(bf16[32,2,64,128]{3,2,1,0:T(8,128)(2,1)} %copy-done.5) | copy-start | bytes 3145732
  20.2 1.6 %copy-start.2 = (f32[2048,256]{1,0:T(8,128)S(1)}, f32[2048,256]{1,0:T(8,128)}, u32[]{:S(2)}) copy-start(f32[2048,256]{1,0:T(8,128)} %copy-done.1) | copy-start | bytes 6291460
  20.2 1.7 %copy-start.4 = (bf16[512,512]{1,0:T(8,128)(2,1)S(1)}, bf16[512,512]{1,0:T(8,128)(2,1)}, u32[]{:S(2)}) copy-start(bf16[512,512]{1,0:T(8,128)(2,1)} %constant.4.clone.dft_ref) | copy-start | bytes 1572868
  24.4 8.2 %collective-permute-start.3 = (bf16[18,2,64,128]{3,2,1,0:T(8,128)(2,1)S(1)}, bf16[18,2,64,128]{3,2,1,0:T(8,128)(2,1)S(1)}, u32[]{:S(2)}, u32[]{:S(2)}) collective-permute-start(bf16[18,2,64,128]{3,2,1,0:T(8,128)(2,1)S(1)} %get-tuple-element.27), channel_id=1, source_target_pairs={{0,1},{1,0},{2,3},{3,2},{4,5},{5,4},{6,7},{7,6},{8,9},{9,8},{10,11... | collective-permute-start | bytes 1769480 | tf_op jit(solution)/shard_map/ppermute | solution.py:307
  34.2 11.3 %collective-permute-start.4 = (f32[8,80,128]{2,1,0:T(8,128)S(1)}, f32[8,80,128]{2,1,0:T(8,128)S(1)}, u32[]{:S(2)}, u32[]{:S(2)}) collective-permute-start(f32[8,80,128]{2,1,0:T(8,128)S(1)} %get-tuple-element.28), channel_id=1, source_target_pairs={{0,2},{1,3},{2,0},{3,1},{4,6},{5,7},{6,4},{7,5},{8,10},{9,11},{10,... | collective-permute-start | bytes 983048 | tf_op jit(solution)/shard_map/ppermute | solution.py:307
  37.3 10.4 %collective-permute-start.5 = (f32[8,80,128]{2,1,0:T(8,128)S(1)}, f32[8,80,128]{2,1,0:T(8,128)S(1)}, u32[]{:S(2)}, u32[]{:S(2)}) collective-permute-start(f32[8,80,128]{2,1,0:T(8,128)S(1)} %get-tuple-element.29), channel_id=1, source_target_pairs={{0,4},{1,5},{2,6},{3,7},{4,0},{5,1},{6,2},{7,3},{8,12},{9,13},{10,... | collective-permute-start | bytes 983048 | tf_op jit(solution)/shard_map/ppermute | solution.py:307
  47.7 5.7 %collective-permute-start.6 = (f32[4,80,128]{2,1,0:T(8,128)S(1)}, f32[4,80,128]{2,1,0:T(8,128)S(1)}, u32[]{:S(2)}, u32[]{:S(2)}) collective-permute-start(f32[4,80,128]{2,1,0:T(8,128)S(1)} %get-tuple-element.30), channel_id=1, source_target_pairs={{0,4},{1,5},{2,6},{3,7},{4,0},{5,1},{6,2},{7,3},{8,12},{9,13},{10,... | collective-permute-start | bytes 491528 | tf_op jit(solution)/shard_map/ppermute | solution.py:307
  49.5 5.3 %collective-permute-start.7 = (f32[4,80,128]{2,1,0:T(8,128)S(1)}, f32[4,80,128]{2,1,0:T(8,128)S(1)}, u32[]{:S(2)}, u32[]{:S(2)}) collective-permute-start(f32[4,80,128]{2,1,0:T(8,128)S(1)} %get-tuple-element.31), channel_id=1, source_target_pairs={{0,2},{1,3},{2,0},{3,1},{4,6},{5,7},{6,4},{7,5},{8,10},{9,11},{10,... | collective-permute-start | bytes 491528 | tf_op jit(solution)/shard_map/ppermute | solution.py:307
  54.9 11.1 %copy-start.8 = (f32[8,128]{1,0:T(8,128)S(1)}, f32[8,128]{1,0:T(8,128)}, u32[]{:S(2)}) copy-start(f32[8,128]{1,0:T(8,128)} %constant.5.clone.steer_ref) | copy-start | bytes 12292
  54.9 6.4 %collective-permute-start.10 = (f32[160,128]{1,0:T(8,128)S(1)}, f32[160,128]{1,0:T(8,128)S(1)}, u32[]{:S(2)}, u32[]{:S(2)}) collective-permute-start(f32[160,128]{1,0:T(8,128)S(1)} %get-tuple-element.34), channel_id=1, source_target_pairs={{0,24},{1,25},{2,26},{3,27},{4,28},{5,29},{6,30},{7,31},{8,16},{9,... | collective-permute-start | bytes 245768 | tf_op jit(solution)/shard_map/ppermute | solution.py:307
  56.5 5.9 %collective-permute-start.8 = (f32[160,128]{1,0:T(8,128)S(1)}, f32[160,128]{1,0:T(8,128)S(1)}, u32[]{:S(2)}, u32[]{:S(2)}) collective-permute-start(f32[160,128]{1,0:T(8,128)S(1)} %get-tuple-element.32), channel_id=1, source_target_pairs={{0,8},{1,9},{2,10},{3,11},{4,12},{5,13},{6,14},{7,15},{8,0},{9,1},... | collective-permute-start | bytes 245768 | tf_op jit(solution)/shard_map/ppermute | solution.py:307
  58.1 32.2 %copy-start.7 = (bf16[32,2,64,128]{3,2,1,0:T(8,128)(2,1)S(1)}, bf16[32,2,64,128]{3,2,1,0:T(8,128)(2,1)}, u32[]{:S(2)}) copy-start(bf16[32,2,64,128]{3,2,1,0:T(8,128)(2,1)} %copy-done.5) | copy-start | bytes 3145732
  58.1 32.2 %copy-start.10 = (s32[32]{0:T(128)S(1)}, s32[32]{0:T(128)}, u32[]{:S(2)}) copy-start(s32[32]{0:T(128)} %bin_ref.1) | copy-start | bytes 388
  58.1 32.2 %copy-start.11 = (s32[32]{0:T(128)S(1)}, s32[32]{0:T(128)}, u32[]{:S(2)}) copy-start(s32[32]{0:T(128)} %block_ref.1) | copy-start | bytes 388
  58.1 32.2 %copy-start.12 = (s32[32]{0:T(128)S(1)}, s32[32]{0:T(128)}, u32[]{:S(2)}) copy-start(s32[32]{0:T(128)} %beam_ref.1) | copy-start | bytes 388
  58.1 32.2 %copy-start.13 = (s32[32,1]{0,1:T(1,128)S(1)}, s32[32,1]{0,1:T(1,128)}, u32[]{:S(2)}) copy-start(s32[32,1]{0,1:T(1,128)} %param.13) | copy-start | bytes 388
  58.1 7.2 %collective-permute-start.9 = (f32[160,128]{1,0:T(8,128)S(1)}, f32[160,128]{1,0:T(8,128)S(1)}, u32[]{:S(2)}, u32[]{:S(2)}) collective-permute-start(f32[160,128]{1,0:T(8,128)S(1)} %get-tuple-element.33), channel_id=1, source_target_pairs={{0,16},{1,17},{2,18},{3,19},{4,20},{5,21},{6,22},{7,23},{8,24},{9,... | collective-permute-start | bytes 245768 | tf_op jit(solution)/shard_map/ppermute | solution.py:307
  65.4 4.6 %collective-permute-start.11 = (f32[160,128]{1,0:T(8,128)S(1)}, f32[160,128]{1,0:T(8,128)S(1)}, u32[]{:S(2)}, u32[]{:S(2)}) collective-permute-start(f32[160,128]{1,0:T(8,128)S(1)} %get-tuple-element.35.own_ref), channel_id=1, source_target_pairs={{0,2},{1,0},{2,6},{3,1},{4,12},{5,7},{6,4},{7,3},{8,16},{9,11},{10... | collective-permute-start | bytes 245768 | tf_op jit(solution)/shard_map/ppermute | solution.py:416
  65.5 4.5 %collective-permute-start.12 = (f32[32,128]{1,0:T(8,128)S(1)}, f32[32,128]{1,0:T(8,128)S(1)}, u32[]{:S(2)}, u32[]{:S(2)}) collective-permute-start(f32[32,128]{1,0:T(8,128)S(1)} %get-tuple-element.36.packed_ref), channel_id=1, source_target_pairs={{0,1},{1,3},{2,0},{3,7},{4,6},{5,13},{6,2},{7,5},{8,10},{9,17},{10... | collective-permute-start | bytes 49160 | tf_op jit(solution)/shard_map/ppermute | solution.py:416
  (3 other events, 2.7 us)
